TPU v7x, 128 devices: a whole 4x4x4 slice. The times are simulated.
128 devices in a mesh: section: 8 (over z_hi, x), peer: 16 (over z_lo, y, core).
Axes of the slice: x: 4, y: 4, z: 4 (z_hi: 2, z_lo: 2; z = z_hi * 2 + z_lo), core: 2. Of those that a mesh axis runs over, the one named last changes fastest.
Arguments:
- acts: bfloat16 [4096, 5120], P('section', 'peer'), may hold values from -50 to 50
- grad_out: bfloat16 [4096, 5120], P('section', 'peer'), may hold values from -6 to 6
- gain: bfloat16 [8, 5120], P('section', 'peer'), may hold values from 0.099609375 to 1.8984375
- w_up: bfloat16 [8, 5120, 10240], P('section', None, 'peer'), may hold values from -0.078125 to 0.078125
- w_down: bfloat16 [8, 10240, 5120], P('section', 'peer'), may hold values from -0.0625 to 0.0625
- senders: int32 [128, 1], replicated, may hold values from 0 to 15; in each aligned block of 16 rows (0 to 15, 16 to 31, ...) at most 2 rows name the same one
- live: int32 [8], P('section'), may hold values from 1 to 16
Outputs:
- grad_up: bfloat16 [8, 5120, 10240], P('section', None, 'peer')
- returned: bfloat16 [8192, 5120], P(('section', 'peer'))
Inputs may be any that keep to these rules, and one draw needn't show every extreme that they name: `senders`: in each section's 16 rows no peer is named more than 2 times, a bound that some block reaches.
All inputs are finite; a program needn't handle non-finite values.
Results may differ from a plain program's by a relative error of at most 0.0065.
Values may be sent and summed in bfloat16 or wider, within the bound.
A program may use at most 128 MiB of HBM per device.

v0:
```python
import jax
import jax.numpy as jnp
from jax import lax
from jax.sharding import PartitionSpec as P

MB = 16
MB_TOK = 32
CAP = 2


def passed_along(x, axis, by):
    length = lax.axis_size(axis)
    pairs = [(i, i + by) for i in range(length) if 0 <= i + by < length]
    return lax.ppermute(x, axis, pairs)


def norm_back(summed, normed, gain_f, rstd, grad_rows):
    scaled_grad = summed * gain_f
    first = jnp.mean(scaled_grad, axis=-1, keepdims=True)
    second = jnp.mean(scaled_grad * normed, axis=-1, keepdims=True)
    total = rstd * (scaled_grad - first - normed * second) + grad_rows.astype(jnp.float32)
    return total.astype(jnp.bfloat16)


def slot_index(section_list):
    same = section_list[:, None] == section_list[None, :]
    earlier = jnp.arange(MB)[None, :] < jnp.arange(MB)[:, None]
    rank = jnp.sum((same & earlier).astype(jnp.int32), axis=1)
    return section_list * CAP + rank


def section_shift(compact):
    return passed_along(compact, "section", -1)


def body(acts, grad_out, gain, w_up, w_down, senders, live):
    acts_full, grad_full, gain_full = (
        lax.all_gather(acts, "peer", axis=1, tiled=True),
        lax.all_gather(grad_out, "peer", axis=1, tiled=True),
        lax.all_gather(gain, "peer", axis=1, tiled=True),
    )
    rows = acts_full.shape[0]
    column = lax.axis_index("peer")
    section = lax.axis_index("section")
    alive = (jnp.arange(rows) // MB_TOK < live[0]).astype(jnp.float32)[:, None]
    values = acts_full.astype(jnp.float32)
    mean = jnp.mean(values, axis=-1, keepdims=True)
    centre = values - mean
    rstd = lax.rsqrt(jnp.mean(centre * centre, axis=-1, keepdims=True) + 1e-05)
    normed = centre * rstd
    gain_f = gain_full.astype(jnp.float32)
    scaled = (normed * gain_f).astype(jnp.bfloat16)
    grad_live = (grad_full.astype(jnp.float32) * alive).astype(jnp.bfloat16)
    up_local = w_up[0]
    down_local = w_down[0]
    pre = jnp.dot(scaled, up_local, preferred_element_type=jnp.float32)
    slope = (
        0.5 * (1.0 + lax.erf(pre * 0.7071067811865476))
        + pre * jnp.exp(-0.5 * pre * pre) * 0.3989422804014327
    )
    back_hidden = lax.dot_general(
        grad_live, down_local, (((1,), (1,)), ((), ())), preferred_element_type=jnp.float32
    )
    back_pre = (back_hidden * slope).astype(jnp.bfloat16)
    count = live[0].astype(jnp.float32)
    grad_up = lax.dot_general(
        scaled, back_pre, (((0,), (0,)), ((), ())), preferred_element_type=jnp.float32
    )
    grad_up = (grad_up / count).astype(jnp.bfloat16)[None]
    section_list = lax.dynamic_slice_in_dim(senders[:, 0], section * MB, MB)
    slots = CAP * MB_TOK
    target = slot_index(section_list)

    def routed_index(start, count_rows):
        index = start + jnp.arange(count_rows)
        wanted = index // MB_TOK
        hit = target[None, :] == wanted[:, None]
        batch = jnp.sum(hit.astype(jnp.int32) * jnp.arange(MB)[None, :], axis=1)
        valid = jnp.any(hit, axis=1)
        return (batch * MB_TOK + index % MB_TOK, valid)

    picked, valid = routed_index(jnp.int32(0), lax.axis_size("peer") * slots)
    piece = jnp.take(back_pre, picked, axis=0)
    summed = lax.psum_scatter(
        (
            lax.dot_general(
                piece, up_local, (((1,), (1,)), ((), ())), preferred_element_type=jnp.float32
            )
            * valid[:, None].astype(jnp.float32)
        ).astype(jnp.bfloat16),
        "peer",
        scatter_dimension=0,
        tiled=True,
    ).astype(jnp.float32)
    picked, valid = routed_index(column * slots, slots)
    grad_rows = jnp.take(grad_live, picked, axis=0) * valid[:, None].astype(jnp.bfloat16)
    compact = norm_back(
        summed, jnp.take(normed, picked, axis=0), gain_f, jnp.take(rstd, picked, axis=0), grad_rows
    )
    returned = section_shift(compact)
    return (grad_up, returned)


def solution(mesh):
    in_specs = (
        P("section", "peer"),
        P("section", "peer"),
        P("section", "peer"),
        P("section", None, "peer"),
        P("section", "peer", None),
        P(),
        P("section"),
    )
    out_specs = (P("section", None, "peer"), P(("section", "peer"), None))
    return jax.shard_map(body, mesh=mesh, in_specs=in_specs, out_specs=out_specs, check_vma=False)
```

profile of v0, /device:TPU:7, one launch (start us, length us, event | category | flops | bytes accessed | tf_op | source)
XLA Modules:
  0.0 242.6 jit_solution(239526053155518608)
XLA Ops:
  8.7 1.2 dynamic-slice.1
  11.6 53.5 %all-reduce = bf16[5120]{0:T(1024)(128)(2,1)S(1)} all-reduce(bf16[5120]{0:T(1024)(128)(2,1)S(1)} %dynamic-update-slice), channel_id=1, replica_groups=mesh['section'=8,'peer'=16] {'peer'}, use_global_device_ids=true, to_apply=%add | all-reduce | flops 5120 | bytes 20480
  65.7 0.7 dynamic-slice_bitcast_fusion
  67.7 8.0 %copy.15 = bf16[512,5120]{1,0:T(8,128)(2,1)} copy(bf16[512,5120]{0,1:T(8,128)(2,1)} %all-gather.3.cloned.1.call-done) | data formatting | bytes 10485760 | tf_op jit(solution)/shard_map/all_gather | solution.py:38
  75.7 3.5 %convert_reduce_fusion = f32[512]{0:T(512)S(1)} fusion(bf16[512,5120]{1,0:T(8,128)(2,1)} %copy.15), kind=kLoop, calls=%fused_computation.7 | loop fusion | flops 5242368 | bytes 5244928 | tf_op jit(solution)/shard_map/reduce_sum | solution.py:47
  79.9 1.5 fusion.2
  81.4 11.8 %all-gather.5.cloned.1.call-done = bf16[512,5120]{0,1:T(8,128)(2,1)} async-done(((bf16[512,320]{0,1:T(8,128)(2,1)}), bf16[512,5120]{0,1:T(8,128)(2,1)}) %all-gather.5.cloned.1.call-update) | async-done | bytes 5242896 | tf_op jit(solution)/shard_map/all_gather | solution.py:39
  93.2 7.9 %copy.16 = bf16[512,5120]{1,0:T(8,128)(2,1)} copy(bf16[512,5120]{0,1:T(8,128)(2,1)} %all-gather.5.cloned.1.call-done) | data formatting | bytes 10485760 | tf_op jit(solution)/shard_map/all_gather | solution.py:39
  101.1 4.3 %multiply_convert_fusion.1 = bf16[512,5120]{1,0:T(8,128)(2,1)S(1)} fusion(bf16[512,5120]{1,0:T(8,128)(2,1)} %copy.16, f32[512]{0:T(512)S(1)} %fusion.38), kind=kLoop, calls=%fused_computation.11 | loop fusion | flops 7864320 | bytes 10487808 | tf_op jit(solution)/shard_map/convert_element_type | solution.py:53
  105.4 10.3 %fusion.4 = f32[512,640]{1,0:T(8,128)S(1)} fusion(bf16[1,5120,640]{2,1,0:T(8,128)(2,1)} %param.10, f32[5120]{0:T(1024)S(1)} %mul.216, bf16[512,5120]{1,0:T(8,128)(2,1)} %copy.15, f32[512]{0:T(512)S(1)} %add_rsqrt_fusion, f32[512]{0:T(512)S(1)} %broadcast_multiply_fusion.1), kind=kOutput, calls=%fused_computation.14 | convolution fusion | flops 3368550400 | bytes 13131776 | tf_op jit(solution)/shard_map/dot_general | solution.py:56
  115.8 4.5 %fusion.12 = bf16[512,640]{1,0:T(8,128)(2,1)S(1)} fusion(bf16[512,5120]{1,0:T(8,128)(2,1)S(1)} %multiply_convert_fusion.1, bf16[1,640,5120]{2,1,0:T(8,128)(2,1)S(1)} %bitcast.35, f32[512,640]{1,0:T(8,128)S(1)} %fusion.4), kind=kOutput, calls=%fused_computation.21 | convolution fusion | flops 3358720000 | bytes 13762560 | tf_op jit(solution)/shard_map/dot_general | solution.py:61
  120.2 4.0 %gather_fusion.1 = bf16[1024,640]{1,0:T(8,128)(2,1)S(1)} fusion(bf16[512,640]{1,0:T(8,128)(2,1)S(1)} %fusion.12, s32[1024]{0:T(1024)S(1)} %broadcast_clamp_fusion), kind=kCustom, calls=%fused_computation.1 | custom fusion | bytes 2625536 | tf_op jit(solution)/shard_map/jit(_take)/gather | solution.py:83
  124.3 14.1 %multiply_convert_fusion = bf16[1024,5120]{1,0:T(8,128)(2,1)} fusion(f32[1024]{0:T(1024)S(1)} %convert_element_type.71, bf16[1,5120,640]{2,1,0:T(8,128)(2,1)} %param.10, bf16[1024,640]{1,0:T(8,128)(2,1)S(1)} %gather_fusion.1, pred[1024]{0:T(1024)(128)(4,1)S(1)} %compare_and_fusion), kind=kOutput, calls=%fused_computation.4 | convolution fusion | flops 6722027520 | bytes 18355200 | tf_op jit(solution)/shard_map/dot_general | solution.py:86
  138.6 0.8 gather_fusion
  139.4 4.7 %gather_fusion.3 = bf16[64,5120]{1,0:T(8,128)(2,1)S(1)} fusion(bf16[512,5120]{1,0:T(8,128)(2,1)} %copy-done.1, s32[1024]{0:T(1024)S(1)} %pad_clamp_fusion), kind=kCustom, calls=%fused_computation.3 | custom fusion | bytes 1310976 | tf_op jit(solution)/shard_map/jit(_take)/gather | solution.py:96
  144.2 8.3 %fusion = f32[512,5120]{1,0:T(8,128)} fusion(bf16[512,5120]{1,0:T(8,128)(2,1)} %copy.15, f32[512]{0:T(512)S(1)} %add_rsqrt_fusion, f32[512]{0:T(512)S(1)} %broadcast_multiply_fusion.1), kind=kLoop, calls=%fused_computation.8 | loop fusion | flops 7864320 | bytes 15732736 | tf_op jit(solution)/shard_map/mul | solution.py:50
  152.4 5.8 %gather_fusion.2 = f32[64,5120]{1,0:T(8,128)S(1)} fusion(f32[512,5120]{1,0:T(8,128)} %fusion, s32[1024]{0:T(1024)S(1)} %pad_clamp_fusion), kind=kCustom, calls=%fused_computation.2 | custom fusion | bytes 2621696 | tf_op jit(solution)/shard_map/jit(_take)/gather | solution.py:98
  158.2 55.7 %reduce-scatter.2.cloned.1.call-done = bf16[64,5120]{1,0:T(8,128)(2,1)} async-done(((bf16[1024,5120]{1,0:T(8,128)(2,1)}), bf16[64,5120]{1,0:T(8,128)(2,1)}) %reduce-scatter.2.cloned.1.call-update) | async-done | bytes 655376 | tf_op jit(solution)/shard_map/reduce_scatter | solution.py:84
  213.9 1.5 fusion.19
  215.4 1.6 add_convert_fusion
  217.1 2.6 %collective-permute-start = (bf16[64,5120]{1,0:T(8,128)(2,1)S(1)}, bf16[64,5120]{1,0:T(8,128)(2,1)S(1)}, u32[]{:S(2)}, u32[]{:S(2)}) collective-permute-start(bf16[64,5120]{1,0:T(8,128)(2,1)S(1)} %add_convert_fusion), channel_id=1, source_target_pairs={{16,0},{32,16},{48,32},{64,48},{80,64},{96,80},{112,96},{17,1},{33... | collective-permute-start | bytes 1966088 | tf_op jit(solution)/shard_map/ppermute | solution.py:14
  219.7 10.1 %fusion.8 = bf16[1,5120,640]{2,1,0:T(8,128)(2,1)} fusion(f32[]{:T(128)S(6)} %convert_element_type.68, bf16[512,640]{1,0:T(8,128)(2,1)S(1)} %fusion.12, f32[5120]{0:T(1024)S(1)} %mul.216, bf16[512,5120]{1,0:T(8,128)(2,1)} %copy.15, f32[512]{0:T(512)S(1)} %add_rsqrt_fusion, f32[512]{0:T(512)S(1)} %broadcast_multiply_fusion.1), kind=kOutput, calls=%fused_computation.18 | convolution fusion | flops 3375104000 | bytes 12476420 | tf_op jit(solution)/shard_map/dot_general | solution.py:66
  229.8 5.4 %collective-permute-done = bf16[64,5120]{1,0:T(8,128)(2,1)S(1)} collective-permute-done((bf16[64,5120]{1,0:T(8,128)(2,1)S(1)}, bf16[64,5120]{1,0:T(8,128)(2,1)S(1)}, u32[]{:S(2)}, u32[]{:S(2)}) %collective-permute-start) | collective-permute-done | bytes 655392 | tf_op jit(solution)/shard_map/ppermute | solution.py:14
  235.2 0.8 copy.20
  (41 shorter events, 4.6 us)
Async XLA Ops:
  7.2 60.5 %all-gather.3.cloned.1.call-start = ((), (), s32[]{:S(2)}) async-start(), calls=%async_computation.1 | async-start | bytes 5570560 | tf_op jit(solution)/shard_map/all_gather | solution.py:38
  7.9 85.3 %all-gather.5.cloned.1.call-start = ((), (), s32[]{:S(2)}) async-start(), calls=%async_computation.2 | async-start | bytes 5570560 | tf_op jit(solution)/shard_map/all_gather | solution.py:39
  8.6 205.3 %reduce-scatter.2.cloned.1.call-start = ((), (), s32[]{:S(2)}) async-start(), calls=%async_computation.3 | async-start | bytes 11141120 | tf_op jit(solution)/shard_map/reduce_scatter | solution.py:84
  75.7 4.2 %copy-start = (bf16[512,5120]{1,0:T(8,128)(2,1)S(1)}, bf16[512,5120]{1,0:T(8,128)(2,1)}, u32[]{:S(2)}) copy-start(bf16[512,5120]{1,0:T(8,128)(2,1)} %copy.15) | copy-start | bytes 15728644
  101.1 14.6 %slice-start = ((s8[6553600]{0:T(1024)(128)(4,1)}), s8[4194304]{0:T(1024)(128)(4,1)S(1)}, s32[]{:S(2)}) async-start(s8[6553600]{0:T(1024)(128)(4,1)} %bitcast.34), calls=%async_computation.4 | async-start | bytes 8388608
  105.4 10.3 %copy-start.1 = (bf16[512,5120]{1,0:T(8,128)(2,1)}, bf16[512,5120]{1,0:T(8,128)(2,1)S(1)}, u32[]{:S(2)}) copy-start(bf16[512,5120]{1,0:T(8,128)(2,1)S(1)} %multiply_convert_fusion.1) | copy-start | bytes 15728644
  105.4 10.3 %slice-start.1 = ((s8[6553600]{0:T(1024)(128)(4,1)}), s8[2359296]{0:T(1024)(128)(4,1)S(1)}, s32[]{:S(2)}) async-start(s8[6553600]{0:T(1024)(128)(4,1)} %bitcast.34), calls=%async_computation.5 | async-start | bytes 4718592
  217.1 18.1 %collective-permute-start = (bf16[64,5120]{1,0:T(8,128)(2,1)S(1)}, bf16[64,5120]{1,0:T(8,128)(2,1)S(1)}, u32[]{:S(2)}, u32[]{:S(2)}) collective-permute-start(bf16[64,5120]{1,0:T(8,128)(2,1)S(1)} %add_convert_fusion), channel_id=1, source_target_pairs={{16,0},{32,16},{48,32},{64,48},{80,64},{96,80},{112,96},{17,1},{33... | collective-permute-start | bytes 1966088 | tf_op jit(solution)/shard_map/ppermute | solution.py:14
Sparse Core Ops, SparseCore 0:
  9.7 42.1 all-gather.2
  53.6 39.5 all-gather.4
  138.5 75.3 reduce-scatter.1
where the time goes:
time: 247 us; the launch traced here: 243 us
  waiting for transfers between devices  74.2 us (30%)
  blocking collectives  53.5 us (22%)
  matrix products  39 us (16%)
  local copies, waits for them, and re-layouts  35.1 us (14%)
  other arithmetic  22.8 us (9%)
  between operations  15.3 us (6%)
  starting transfers between devices  2.73 us (1%)
    reduce_scatter x1, waiting for transfers between devices, body(): lax.psum_scatter((lax.dot_general(piece, up_local, (((1,), (1,)), ((), ()...  55.7 us
    unnamed x1, blocking collectives  53.5 us
    dot_general x1, matrix products, body(): lax.dot_general(piece, up_local, (((1,), (1,)), ((), ())), preferred_elem...  14.1 us
    all_gather x1, waiting for transfers between devices, body(): lax.all_gather(grad_out, 'peer', axis=1, tiled=True)  11.8 us
    dot_general x1, matrix products, body(): pre = jnp.dot(scaled, up_local, preferred_element_type=jnp.float32)  10.3 us
    dot_general x1, matrix products, body(): lax.dot_general(scaled, back_pre, (((0,), (0,)), ((), ())), preferred_ele...  10.1 us
    mul x1, other arithmetic, body(): normed = centre * rstd  8.25 us
    all_gather x1, local copies, waits for them, and re-layouts, body(): lax.all_gather(acts, 'peer', axis=1, tiled=True)  8.01 us
  transfers between devices with their start and end apart: 4, of which 3 were waited for; matrix products, arithmetic and copies ran while one was open for 19% of the time, Pallas kernels for 0%

commit v1 on v0

v1 whole, which is shorter than its diff:
```python
import functools

import jax
import jax.numpy as jnp
from jax import lax
from jax.experimental import pallas as pl
from jax.experimental.pallas import tpu as pltpu
from jax.sharding import PartitionSpec as P

MESH = pl.DeviceIdType.MESH
F32 = jnp.float32
BF16 = jnp.bfloat16
MB = 16
MB_TOK = 32
ROWS = 512
HALF = 256
QUART = 128
D = 5120
CHIP = 640
LOCAL = 320
CHIPS = 8
MIB = 2**20

MATES = [(0, 1), (0, 2), (0, 3), (1, 0), (1, 1), (1, 2), (1, 3)]
GATHER_ORDER = [(0, 0), (1, 0), (0, 3), (0, 1), (0, 2), (1, 3), (1, 1), (1, 2)]
SUM_ORDER = [(1, 2), (1, 1), (1, 3), (0, 1), (0, 3), (0, 2), (1, 0), (0, 0)]
LAG = 3

N_AG = 19


def nt_dot(a, b):
    return lax.dot_general(a, b, (((1,), (1,)), ((), ())), preferred_element_type=F32)


def pick(table, k):
    out = table[0]
    for i in range(1, len(table)):
        out = jnp.where(k == i, table[i], out)
    return out


def place():
    s = lax.axis_index("section")
    p = lax.axis_index("peer")
    q = p // 2
    return s, q // 4, q % 4, p % 2


def layer_kernel(
    acts_ref, grad_ref, gain_ref, live_ref, wu_hbm, wd_hbm,
    compact_ref, x_hbm, bp_hbm,
    wu, wd, g_all, x_all, pre, bh, bp, part, sib_part, r_a, r_b, r_c, r_e, r_d,
    gl, sib_gl, sib_acts, my_gain, sib_gain, normed, facts, sums, sib_sums,
    all_sums, out_buf,
    ag_send, ag_recv, own_send, own_recv, facts_send, facts_recv, sums_send, sums_recv,
    sib_send, sib_recv, rs_send, rs_recv, local_sem,
):
    s, z, y, c = place()
    z2, yp, ym, y2 = 1 - z, (y + 1) % 4, (y + 3) % 4, (y + 2) % 4
    oc = 1 - c
    q_me = z * 4 + y

    def dev(zz, yy, cc):
        return (s, (zz * 4 + yy) * 2 + cc)

    def rows(lane, half=None):
        if half is None:
            return pl.ds(pl.multiple_of(lane * HALF, HALF), HALF)
        return pl.ds(pl.multiple_of(lane * HALF + half * QUART, QUART), QUART)

    sends = []

    def remote(src, dst, ssem, rsem, where):
        return pltpu.make_async_remote_copy(
            src_ref=src, dst_ref=dst, send_sem=ssem, recv_sem=rsem,
            device_id=where, device_id_type=MESH,
        )

    def send(src, dst, ssem, rsem, where):
        copy = remote(src, dst, ssem, rsem, where)
        copy.start()
        sends.append(copy)

    def recv(dst, ssem, rsem):
        remote(dst, dst, ssem, rsem, dev(z, y, oc)).wait_recv()

    load_wd = pltpu.make_async_copy(wd_hbm.at[0], wd, local_sem.at[0])
    load_wu = pltpu.make_async_copy(wu_hbm.at[0], wu, local_sem.at[1])
    load_wd.start()
    load_wu.start()

    barrier = pltpu.get_barrier_semaphore()
    pl.semaphore_signal(barrier, inc=1, device_id=dev(z, y, oc), device_id_type=MESH)
    for dz, dy in MATES:
        pl.semaphore_signal(
            barrier, inc=1, device_id=dev((z + dz) % 2, (y + dy) % 4, c), device_id_type=MESH
        )
    pl.semaphore_wait(barrier, 8)

    token = lax.broadcasted_iota(jnp.int32, (ROWS, LOCAL), 0) // MB_TOK
    alive = (token < live_ref[0]).astype(F32)
    gl[...] = (grad_ref[...].astype(F32) * alive).astype(BF16)
    send(gl.at[rows(oc)], sib_gl, own_send.at[0], own_recv.at[0], dev(z, y, oc))
    send(acts_ref.at[rows(oc)], sib_acts, own_send.at[1], own_recv.at[1], dev(z, y, oc))
    my_gain[...] = jnp.broadcast_to(gain_ref[...].astype(F32), (8, LOCAL))
    send(my_gain, sib_gain, own_send.at[2], own_recv.at[2], dev(z, y, oc))

    def side_by_side(mine, other):
        left = jnp.where(c == 0, mine, other)
        right = jnp.where(c == 0, other, mine)
        return jnp.concatenate([left, right], axis=1)

    bufs = (g_all, x_all)

    def block(a, zz, yy, lane, half=None):
        return bufs[a].at[zz * 4 + yy, rows(lane, half)]

    def ag_start(a, tag, zz, yy, where, half=None):
        ref = block(a, zz, yy, c, half)
        send(ref, ref, ag_send.at[a, tag], ag_recv.at[a, tag], where)

    def ag_wait(a, tag, zz, yy, lane, half=None):
        recv(block(a, zz, yy, lane, half), ag_send.at[a, tag], ag_recv.at[a, tag])

    def ag_own(a):
        ag_start(a, 0, z, y, dev(z2, y, c))
        ag_start(a, 1, z, y, dev(z, yp, c))
        ag_start(a, 2, z, y, dev(z, ym, c))
        ag_start(a, 9, z, y, dev(z, y, oc))

    def ag_second(a):
        ag_wait(a, 1, z, ym, c)
        ag_start(a, 3, z, ym, dev(z, yp, c), 0)
        ag_wait(a, 2, z, yp, c)
        ag_start(a, 4, z, yp, dev(z, ym, c), 1)
        ag_wait(a, 0, z2, y, c)
        ag_start(a, 5, z2, y, dev(z, yp, c))
        ag_start(a, 6, z2, y, dev(z, ym, c))
        ag_start(a, 10, z, ym, dev(z, y, oc))
        ag_start(a, 11, z, yp, dev(z, y, oc))
        ag_start(a, 12, z2, y, dev(z, y, oc))

    def ag_second_sib(a):
        ag_wait(a, 10, z, ym, oc)
        ag_wait(a, 11, z, yp, oc)
        ag_wait(a, 12, z2, y, oc)

    def ag_third(a):
        ag_wait(a, 3, z, y2, c, 0)
        ag_start(a, 7, z, y2, dev(z2, y, c), 0)
        ag_wait(a, 4, z, y2, c, 1)
        ag_start(a, 8, z, y2, dev(z2, y, c), 1)
        ag_start(a, 13, z, y2, dev(z, y, oc), 0)
        ag_start(a, 14, z, y2, dev(z, y, oc), 1)

    def ag_fourth(a):
        ag_wait(a, 5, z2, ym, c)
        ag_start(a, 15, z2, ym, dev(z, y, oc))
        ag_wait(a, 6, z2, yp, c)
        ag_start(a, 16, z2, yp, dev(z, y, oc))
        ag_wait(a, 7, z2, y2, c, 0)
        ag_start(a, 17, z2, y2, dev(z, y, oc), 0)
        ag_wait(a, 8, z2, y2, c, 1)
        ag_start(a, 18, z2, y2, dev(z, y, oc), 1)

    def ag_fourth_sib(a):
        ag_wait(a, 13, z, y2, oc, 0)
        ag_wait(a, 14, z, y2, oc, 1)
        ag_wait(a, 17, z2, y2, oc, 0)
        ag_wait(a, 18, z2, y2, oc, 1)
        ag_wait(a, 15, z2, ym, oc)
        ag_wait(a, 16, z2, yp, oc)

    def chip_at(table, k):
        dz = pick([t[0] for t in table], k)
        dy = pick([t[1] for t in table], k)
        return ((z + dz) % 2) * 4 + (y + dy) % 4

    def columns(q):
        return pl.ds(pl.multiple_of(q * CHIP, CHIP), CHIP)

    def mul_g(lo, hi):
        @pl.loop(lo, hi)
        def _(k):
            q = chip_at(GATHER_ORDER, k)
            term = nt_dot(g_all[q], wd[:, columns(q)])
            if lo == 0:
                bh[...] = term
            else:
                bh[...] += term

    def mul_x(lo, hi):
        @pl.loop(lo, hi)
        def _(k):
            q = chip_at(GATHER_ORDER, k)
            term = jnp.dot(x_all[q], wu[columns(q), :], preferred_element_type=F32)
            if lo == 0:
                pre[...] = term
            else:
                pre[...] += term

    recv(sib_gl, own_send.at[0], own_recv.at[0])
    g_all[q_me, rows(c)] = side_by_side(
        gl[rows(c)].astype(F32), sib_gl[...].astype(F32)
    ).astype(BF16)
    ag_own(0)

    recv(sib_acts, own_send.at[1], own_recv.at[1])
    recv(sib_gain, own_send.at[2], own_recv.at[2])
    values = side_by_side(acts_ref[rows(c)].astype(F32), sib_acts[...].astype(F32))
    gain_chip = side_by_side(my_gain[...], sib_gain[...])
    mean_here = jnp.mean(values, axis=1, keepdims=True)
    spread = values - mean_here
    square_here = jnp.sum(spread * spread, axis=1, keepdims=True)
    lane_at = lax.broadcasted_iota(jnp.int32, (HALF, 128), 1)
    table = jnp.where(lane_at == 0, mean_here, jnp.where(lane_at == 1, square_here, 0.0))
    facts[q_me, :, 0:HALF] = table.T[0:8]
    facts[q_me, :, HALF:] = gain_chip
    for i, (dz, dy) in enumerate(MATES):
        send(
            facts.at[q_me], facts.at[q_me], facts_send.at[i], facts_recv.at[i],
            dev((z + dz) % 2, (y + dy) % 4, c),
        )
    normed[...] = values

    def columns_of(first_row, second_row):
        tall = jnp.concatenate(
            [first_row, second_row, jnp.zeros((126, HALF), F32)], axis=0
        ).T
        return tall[:, 0:1], tall[:, 1:2]

    for i, (dz, dy) in enumerate(MATES):
        recv(facts.at[((z + dz) % 2) * 4 + (y + 4 - dy) % 4], facts_send.at[i], facts_recv.at[i])
    means = [facts[i, 0:1, 0:HALF] for i in range(CHIPS)]
    mean_row = sum(means) / CHIPS
    square_row = sum(facts[i, 1:2, 0:HALF] for i in range(CHIPS))
    square_row += CHIP * sum((m - mean_row) * (m - mean_row) for m in means)
    rstd_row = lax.rsqrt(square_row / D + 1e-05)
    mean_col, rstd_col = columns_of(mean_row, rstd_row)
    normed[...] = (normed[...] - mean_col) * rstd_col
    x_all[q_me, rows(c)] = (normed[...] * facts[q_me, 0:1, HALF:]).astype(BF16)
    ag_own(1)

    load_wd.wait()
    ag_wait(0, 9, z, y, oc)
    mul_g(0, 1)
    ag_second(0)
    load_wu.wait()
    ag_wait(1, 9, z, y, oc)
    mul_x(0, 1)
    ag_second_sib(0)
    mul_g(1, 4)
    ag_second(1)
    ag_third(0)
    ag_second_sib(1)
    mul_x(1, 4)
    weight_sum = jnp.zeros((16, CHIP), F32)
    for i in range(CHIPS):
        gain_i = jnp.broadcast_to(facts[i, 0:1, HALF:], (16, CHIP)).astype(BF16)
        weight_sum += jnp.dot(gain_i, wu[i * CHIP : (i + 1) * CHIP], preferred_element_type=F32)
    ag_third(1)
    ag_fourth(0)
    ag_fourth_sib(0)
    mul_g(4, 8)
    ag_fourth(1)
    ag_fourth_sib(1)
    mul_x(4, 8)
    save_x = pltpu.make_async_copy(x_all, x_hbm, local_sem.at[2])
    save_x.start()

    weight_row = weight_sum[0:1]

    @pl.loop(0, ROWS // 128)
    def _(i):
        at = pl.ds(pl.multiple_of(i * 128, 128), 128)
        p = pre[at]
        slope = (
            0.5 * (1.0 + lax.erf(p * 0.7071067811865476))
            + p * jnp.exp(-0.5 * p * p) * 0.3989422804014327
        )
        b = (bh[at] * slope).astype(BF16)
        bp[at] = b
        b = b.astype(F32)
        first = jnp.sum(b * weight_row, axis=1, keepdims=True)
        second = jnp.sum(b * p, axis=1, keepdims=True)
        lane = lax.broadcasted_iota(jnp.int32, (128, 128), 1)
        both = jnp.where(lane == 0, first, jnp.where(lane == 1, second, 0.0))
        sums[i // 2, i % 2] = both.T[0:8]

    save_bp = pltpu.make_async_copy(bp, bp_hbm, local_sem.at[3])
    save_bp.start()
    send(sums.at[oc], sib_sums, sums_send.at[7], sums_recv.at[7], dev(z, y, oc))

    def sib_copy(q):
        return remote(
            part.at[q, rows(oc)], sib_part.at[q], sib_send.at[q], sib_recv.at[q], dev(z, y, oc)
        )

    def rs_start(tag, src, dst, where):
        send(src, dst, rs_send.at[tag], rs_recv.at[tag], where)

    def rs_wait(tag, dst):
        recv(dst, rs_send.at[tag], rs_recv.at[tag])

    def chip(zz, yy):
        return zz * 4 + yy

    q_p, q_m, q_2 = chip(z, yp), chip(z, ym), chip(z, y2)
    q_z, q_zp, q_zm, q_z2 = chip(z2, y), chip(z2, yp), chip(z2, ym), chip(z2, y2)
    h0, h1 = pl.ds(0, QUART), pl.ds(QUART, QUART)

    def multiply(k):
        q = chip_at(SUM_ORDER, k)
        part[q] = nt_dot(bp[...], wu[columns(q), :]).astype(BF16)
        sib_copy(q).start()

    def join(k):
        q = chip_at(SUM_ORDER, k)
        sib_copy(q).wait_recv()
        part[q, rows(c)] = (part[q, rows(c)].astype(F32) + sib_part[q].astype(F32)).astype(BF16)

    @pl.loop(0, LAG)
    def _(k):
        multiply(k)

    @pl.loop(LAG, CHIPS)
    def _(k):
        multiply(k)
        join(k - LAG)

        @pl.when(k == LAG)
        def _():
            remote(part.at[q_z2, rows(c)], r_a, rs_send.at[0], rs_recv.at[0], dev(z2, y, c)).start()

        @pl.when(k == LAG + 1)
        def _():
            remote(
                part.at[q_zp, rows(c)], r_b.at[0], rs_send.at[1], rs_recv.at[1], dev(z, yp, c)
            ).start()

        @pl.when(k == LAG + 2)
        def _():
            remote(
                part.at[q_zm, rows(c)], r_b.at[1], rs_send.at[2], rs_recv.at[2], dev(z, ym, c)
            ).start()

        @pl.when(k == LAG + 3)
        def _():
            remote(
                part.at[q_p, rows(c, 1)], r_e.at[0, h1], rs_send.at[3], rs_recv.at[3],
                dev(z, yp, c),
            ).start()

        @pl.when(k == LAG + 4)
        def _():
            remote(
                part.at[q_m, rows(c, 0)], r_e.at[1, h0], rs_send.at[4], rs_recv.at[4],
                dev(z, ym, c),
            ).start()

    @pl.loop(CHIPS - LAG, CHIPS)
    def _(k):
        join(k)

    sends.extend(
        [
            remote(part.at[q_z2, rows(c)], r_a, rs_send.at[0], rs_recv.at[0], dev(z2, y, c)),
            remote(part.at[q_zp, rows(c)], r_b.at[0], rs_send.at[1], rs_recv.at[1], dev(z, yp, c)),
            remote(part.at[q_zm, rows(c)], r_b.at[1], rs_send.at[2], rs_recv.at[2], dev(z, ym, c)),
            remote(part.at[q_p, rows(c, 1)], r_e.at[0, h1], rs_send.at[3], rs_recv.at[3], dev(z, yp, c)),
            remote(part.at[q_m, rows(c, 0)], r_e.at[1, h0], rs_send.at[4], rs_recv.at[4], dev(z, ym, c)),
        ]
    )

    recv(sib_sums, sums_send.at[7], sums_recv.at[7])
    all_sums[q_me] = sums[c] + sib_sums[...]
    for i, (dz, dy) in enumerate(MATES):
        send(
            all_sums.at[q_me], all_sums.at[q_me], sums_send.at[i], sums_recv.at[i],
            dev((z + dz) % 2, (y + dy) % 4, c),
        )

    rs_wait(0, r_a)
    part[q_2, rows(c)] = (part[q_2, rows(c)].astype(F32) + r_a[...].astype(F32)).astype(BF16)
    rs_start(5, part.at[q_2, rows(c, 0)], r_c.at[0], dev(z, yp, c))
    rs_start(6, part.at[q_2, rows(c, 1)], r_c.at[1], dev(z, ym, c))
    rs_wait(1, r_b.at[0])
    rs_wait(2, r_b.at[1])
    part[q_z, rows(c)] = (
        part[q_z, rows(c)].astype(F32) + r_b[0].astype(F32) + r_b[1].astype(F32)
    ).astype(BF16)
    rs_start(7, part.at[q_z, rows(c)], r_d, dev(z2, y, c))
    rs_wait(5, r_c.at[0])
    part[q_p, rows(c, 0)] = (part[q_p, rows(c, 0)].astype(F32) + r_c[0].astype(F32)).astype(BF16)
    rs_start(8, part.at[q_p, rows(c, 0)], r_e.at[0, h0], dev(z, yp, c))
    rs_wait(6, r_c.at[1])
    part[q_m, rows(c, 1)] = (part[q_m, rows(c, 1)].astype(F32) + r_c[1].astype(F32)).astype(BF16)
    rs_start(9, part.at[q_m, rows(c, 1)], r_e.at[1, h1], dev(z, ym, c))

    for i, (dz, dy) in enumerate(MATES):
        recv(
            all_sums.at[((z + dz) % 2) * 4 + (y + 4 - dy) % 4], sums_send.at[i], sums_recv.at[i]
        )
    total_sums = sum(all_sums[i] for i in range(CHIPS)) / D
    row_first = jnp.concatenate([total_sums[0, 0:1], total_sums[1, 0:1]], axis=1)
    row_second = jnp.concatenate([total_sums[0, 1:2], total_sums[1, 1:2]], axis=1)
    first_col, second_col = columns_of(row_first, row_second)

    rs_wait(7, r_d)
    rs_wait(3, r_e.at[0, h1])
    rs_wait(4, r_e.at[1, h0])
    rs_wait(8, r_e.at[0, h0])
    rs_wait(9, r_e.at[1, h1])
    summed = (
        part[q_me, rows(c)].astype(F32)
        + r_d[...].astype(F32)
        + r_e[0].astype(F32)
        + r_e[1].astype(F32)
    )
    scaled_grad = summed * facts[q_me, 0:1, HALF:]
    total = rstd_col * (scaled_grad - first_col - normed[...] * second_col)
    out_buf[...] = (total + g_all[q_me, rows(c)].astype(F32)).astype(BF16)
    save_out = pltpu.make_async_copy(out_buf, compact_ref, local_sem.at[4])
    save_out.start()

    @pl.loop(0, CHIPS)
    def _(k):
        sib_copy(k).wait_send()

    for copy in sends:
        copy.wait_send()
    save_x.wait()
    save_bp.wait()
    save_out.wait()


def layer(acts, grad_out, gain, live, w_up, w_down):
    vmem, anyspace = pl.BlockSpec(memory_space=pltpu.VMEM), pl.BlockSpec(memory_space=pl.ANY)
    dma = pltpu.SemaphoreType.DMA
    return pl.pallas_call(
        layer_kernel,
        out_shape=[
            jax.ShapeDtypeStruct((HALF, CHIP), BF16),
            jax.ShapeDtypeStruct((CHIPS, ROWS, CHIP), BF16),
            jax.ShapeDtypeStruct((ROWS, CHIP), BF16),
        ],
        in_specs=[vmem, vmem, vmem, pl.BlockSpec(memory_space=pltpu.SMEM), anyspace, anyspace],
        out_specs=[anyspace, anyspace, anyspace],
        scratch_shapes=[
            pltpu.VMEM((D, CHIP), BF16),
            pltpu.VMEM((CHIP, D), BF16),
            pltpu.VMEM((CHIPS, ROWS, CHIP), BF16),
            pltpu.VMEM((CHIPS, ROWS, CHIP), BF16),
            pltpu.VMEM((ROWS, CHIP), F32),
            pltpu.VMEM((ROWS, CHIP), F32),
            pltpu.VMEM((ROWS, CHIP), BF16),
            pltpu.VMEM((CHIPS, ROWS, CHIP), BF16),
            pltpu.VMEM((CHIPS, HALF, CHIP), BF16),
            pltpu.VMEM((HALF, CHIP), BF16),
            pltpu.VMEM((2, HALF, CHIP), BF16),
            pltpu.VMEM((2, QUART, CHIP), BF16),
            pltpu.VMEM((2, HALF, CHIP), BF16),
            pltpu.VMEM((HALF, CHIP), BF16),
            pltpu.VMEM((ROWS, LOCAL), BF16),
            pltpu.VMEM((HALF, LOCAL), BF16),
            pltpu.VMEM((HALF, LOCAL), BF16),
            pltpu.VMEM((8, LOCAL), F32),
            pltpu.VMEM((8, LOCAL), F32),
            pltpu.VMEM((HALF, CHIP), F32),
            pltpu.VMEM((CHIPS, 8, HALF + CHIP), F32),
            pltpu.VMEM((2, 2, 8, 128), F32),
            pltpu.VMEM((2, 8, 128), F32),
            pltpu.VMEM((CHIPS, 2, 8, 128), F32),
            pltpu.VMEM((HALF, CHIP), BF16),
            dma((2, N_AG)),
            dma((2, N_AG)),
            dma((3,)),
            dma((3,)),
            dma((7,)),
            dma((7,)),
            dma((8,)),
            dma((8,)),
            dma((CHIPS,)),
            dma((CHIPS,)),
            dma((10,)),
            dma((10,)),
            dma((5,)),
        ],
        compiler_params=pltpu.CompilerParams(
            collective_id=0, has_side_effects=True, vmem_limit_bytes=56 * MIB
        ),
        cost_estimate=pl.CostEstimate(
            flops=6 * ROWS * D * CHIP, bytes_accessed=20 * MIB, transcendentals=2 * ROWS * CHIP
        ),
    )(acts, grad_out, gain, live, w_up, w_down)


def route_kernel(
    compact_ref, senders_ref, out_ref,
    full, stage, landed,
    sib_send, sib_recv, put_send, put_recv,
):
    s, z, y, c = place()
    oc = 1 - c
    q_me = z * 4 + y

    def dev(zz, yy, cc):
        return (s, (zz * 4 + yy) * 2 + cc)

    def remote(src, dst, ssem, rsem, where):
        return pltpu.make_async_remote_copy(
            src_ref=src, dst_ref=dst, send_sem=ssem, recv_sem=rsem,
            device_id=where, device_id_type=MESH,
        )

    barrier = pltpu.get_barrier_semaphore()
    pl.semaphore_signal(barrier, inc=1, device_id=dev(z, y, oc), device_id_type=MESH)
    for dz, dy in MATES:
        pl.semaphore_signal(
            barrier, inc=1, device_id=dev((z + dz) % 2, (y + dy) % 4, c), device_id_type=MESH
        )
    pl.semaphore_wait(barrier, 8)

    mine = pl.ds(pl.multiple_of(c * HALF, HALF), HALF)
    other = pl.ds(pl.multiple_of(oc * HALF, HALF), HALF)
    sib = remote(compact_ref, full.at[mine], sib_send, sib_recv, dev(z, y, oc))
    sib.start()
    full[mine] = compact_ref[...]

    base = jnp.minimum(s + 1, lax.axis_size("section") - 1) * MB
    names = [senders_ref[base + m] for m in range(MB)]

    token = lax.broadcasted_iota(jnp.int32, (2 * MB_TOK, ROWS), 1)
    slot_row = token % MB_TOK
    for m in range(MB):
        rank = jnp.int32(0)
        for before in range(m):
            rank = rank + jnp.where(names[before] == names[m], 1, 0)
        slot_row += jnp.where(token // MB_TOK == m, (names[m] * 2 + rank) * MB_TOK, 0)
    row = lax.broadcasted_iota(jnp.int32, (2 * MB_TOK, ROWS), 0)

    remote(full.at[other], full.at[other], sib_send, sib_recv, dev(z, y, oc)).wait_recv()

    def fill(dz, dy):
        peer = (((z + dz) % 2) * 4 + (y + dy) % 4) * 2 + c
        chosen = jnp.where(slot_row == row + peer * (2 * MB_TOK), 1.0, 0.0).astype(BF16)
        return jnp.dot(chosen, full[...], preferred_element_type=F32).astype(BF16)

    puts = []
    columns = pl.ds(pl.multiple_of(q_me * CHIP, CHIP), CHIP)
    for i, (dz, dy) in enumerate(MATES):
        stage[i] = fill(dz, dy)
        put = remote(
            stage.at[i], landed.at[:, columns], put_send.at[i], put_recv.at[i],
            dev((z + dz) % 2, (y + dy) % 4, c),
        )
        put.start()
        puts.append(put)
    landed[:, columns] = fill(0, 0)
    for i, (dz, dy) in enumerate(MATES):
        q = ((z + dz) % 2) * 4 + (y + 4 - dy) % 4
        there = landed.at[:, pl.ds(pl.multiple_of(q * CHIP, CHIP), CHIP)]
        remote(there, there, put_send.at[i], put_recv.at[i], dev(z, y, oc)).wait_recv()
    out_ref[...] = landed[...]
    sib.wait_send()
    for put in puts:
        put.wait_send()


def route(compact, senders):
    vmem = pl.BlockSpec(memory_space=pltpu.VMEM)
    dma = pltpu.SemaphoreType.DMA
    return pl.pallas_call(
        route_kernel,
        out_shape=jax.ShapeDtypeStruct((2 * MB_TOK, D), BF16),
        in_specs=[vmem, pl.BlockSpec(memory_space=pltpu.SMEM)],
        out_specs=vmem,
        scratch_shapes=[
            pltpu.VMEM((ROWS, CHIP), BF16),
            pltpu.VMEM((7, 2 * MB_TOK, CHIP), BF16),
            pltpu.VMEM((2 * MB_TOK, D), BF16),
            dma,
            dma,
            dma((7,)),
            dma((7,)),
        ],
        compiler_params=pltpu.CompilerParams(
            collective_id=1, has_side_effects=True, vmem_limit_bytes=16 * MIB
        ),
    )(compact, senders)


def body(acts, grad_out, gain, w_up, w_down, senders, live):
    compact, scaled, back_pre = layer(acts, grad_out, gain, live, w_up, w_down)
    length = lax.axis_size("section")
    shifted = lax.ppermute(compact, "section", [(i, i - 1) for i in range(1, length)])
    grad_up = lax.dot_general(
        scaled, back_pre, (((1,), (0,)), ((), ())), preferred_element_type=F32
    ).reshape(D, CHIP)
    grad_up = (grad_up / live[0].astype(F32)).astype(BF16)[None]
    returned = route(shifted, senders[:, 0])
    return (grad_up, returned)


def solution(mesh):
    in_specs = (
        P("section", "peer"),
        P("section", "peer"),
        P("section", "peer"),
        P("section", None, "peer"),
        P("section", "peer", None),
        P(),
        P("section"),
    )
    out_specs = (P("section", None, "peer"), P(("section", "peer"), None))
    return jax.shard_map(body, mesh=mesh, in_specs=in_specs, out_specs=out_specs, check_vma=False)
```

time: 247 us -> 123 us (0.50); the launches traced: 243 us -> 123 us
  Pallas kernels: 0 us -> 103 us
  waiting for transfers between devices: 74.2 us -> 1.92 us
  blocking collectives: 53.5 us -> 0 us
  local copies, waits for them, and re-layouts: 35.1 us -> 4.63 us
  matrix products: 39 us -> 9.73 us
  other arithmetic: 22.8 us -> 0 us
  between operations: 15.3 us -> 1.32 us
    pallas_call x0 -> x2, Pallas kernels: none -> 103 us  [the longest x1 85.6 us: layer(): pl.pallas_call(layer_kernel, out_shape=[jax.ShapeDtypeStruct((HALF, CHIP)...]
    reduce_scatter x1 -> x0, waiting for transfers between devices: 55.7 us -> none  [body(): lax.psum_scatter((lax.dot_general(piece, up_local, (((1,), (1,)), ((), ()...]
    unnamed x1 -> x0, blocking collectives: 53.5 us -> none
    dot_general x4 -> x1, matrix products: 39 us -> 9.73 us  [body(): lax.dot_general(scaled, back_pre, (((1,), (0,)), ((), ())), preferred_ele...]
    all_gather x2 -> x0, local copies, waits for them, and re-layouts: 15.9 us -> none  [the longest x1 8.01 us: body(): lax.all_gather(acts, 'peer', axis=1, tiled=True)]
    gather x4 -> x0, local copies, waits for them, and re-layouts: 15.3 us -> none  [the longest x1 5.78 us: body(): jnp.take(normed, picked, axis=0)]
    all_gather x2 -> x0, waiting for transfers between devices: 11.8 us -> none  [the longest x1 11.8 us: body(): lax.all_gather(grad_out, 'peer', axis=1, tiled=True)]
    mul x3 -> x0, other arithmetic: 8.26 us -> none  [the longest x1 8.25 us: body(): normed = centre * rstd]
  transfers between devices with their start and end apart: 4 -> 1, of which waited for: 3 -> 1; matrix products, arithmetic and copies ran while one was open for 19% -> 8% of each run, Pallas kernels for 0% -> 0%
where the time goes in v1:
time: 123 us
  Pallas kernels  103 us (84%)
  matrix products  9.73 us (8%)
  local copies, waits for them, and re-layouts  4.63 us (4%)
  starting transfers between devices  2.66 us (2%)
  waiting for transfers between devices  1.92 us (2%)
  between operations  1.32 us (1%)
    pallas_call x1, Pallas kernels, layer(): pl.pallas_call(layer_kernel, out_shape=[jax.ShapeDtypeStruct((HALF, CHIP)...  85.6 us
    pallas_call x1, Pallas kernels, route(): pl.pallas_call(route_kernel, out_shape=jax.ShapeDtypeStruct((2 * MB_TOK,...  17.1 us
    dot_general x1, matrix products, body(): lax.dot_general(scaled, back_pre, (((1,), (0,)), ((), ())), preferred_ele...  9.73 us
    unnamed x5, local copies, waits for them, and re-layouts  4.63 us
    ppermute x1, starting transfers between devices, body(): lax.ppermute(compact, 'section', [(i, i - 1) for i in range(1, length)])  2.66 us
  transfers between devices with their start and end apart: 1, of which 1 were waited for; matrix products, arithmetic and copies ran while one was open for 8% of the time, Pallas kernels for 0%

profile of v1, /device:TPU:7, one launch (start us, length us, event | category | flops | bytes accessed | tf_op | source)
XLA Modules:
  0.0 122.9 jit_solution(273516914637090295)
XLA Ops:
  1.3 1.9 %copy.10.grad_ref = bf16[512,320]{1,0:T(8,128)(2,1)} copy(bf16[512,320]{0,1:T(8,128)(2,1)} %param.8) | data formatting | bytes 655360 | tf_op args[1]
  3.2 1.9 %copy.9.acts_ref = bf16[512,320]{1,0:T(8,128)(2,1)} copy(bf16[512,320]{0,1:T(8,128)(2,1)} %param.7) | data formatting | bytes 655360 | tf_op args[0]
  5.1 85.6 %shard_map.86 = (bf16[256,640]{1,0:T(8,128)(2,1)}, bf16[8,512,640]{2,1,0:T(8,128)(2,1)}, bf16[512,640]{1,0:T(8,128)(2,1)}) custom-call(bf16[512,320]{1,0:T(8,128)(2,1)} %copy.9.acts_ref, bf16[512,320]{1,0:T(8,128)(2,1)} %copy.10.grad_ref, bf16[1,320]{1,0:T(2,128)(2,1)} %gain_ref.1, s32[1]{0:T(128)S(6)} %copy.14.live_ref, bf16[1,5120,640]{2,1,0:T(8,128)(2,1)} %wu_hbm.1, ...), custom_call_target="tpu_custom_call" | custom-call | flops 10066329600 | bytes 20971520 | tf_op jit(solution)/shard_map/pallas_call | solution.py:441
  90.6 2.7 %collective-permute-start = (bf16[256,640]{1,0:T(8,128)(2,1)}, bf16[256,640]{1,0:T(8,128)(2,1)S(1)}, u32[]{:S(2)}, u32[]{:S(2)}) collective-permute-start(bf16[256,640]{1,0:T(8,128)(2,1)} %get-tuple-element.7), channel_id=1, source_target_pairs={{16,0},{32,16},{48,32},{64,48},{80,64},{96,80},{112,96},{17,1},{33... | collective-permute-start | bytes 983048 | tf_op jit(solution)/shard_map/ppermute | solution.py:597
  93.3 0.0 copy-start
  93.3 9.7 %divide_convert_fusion = bf16[8,640,640]{2,1,0:T(8,128)(2,1)} fusion(bf16[8,512,640]{2,1,0:T(8,128)(2,1)} %get-tuple-element.5, f32[]{:T(128)} %bitcast.1, bf16[512,640]{1,0:T(8,128)(2,1)} %get-tuple-element.6), kind=kOutput, calls=%fused_computation | convolution fusion | flops 3361996800 | bytes 12451844 | tf_op jit(solution)/shard_map/dot_general | solution.py:598
  103.0 1.9 %collective-permute-done.compact_ref = bf16[256,640]{1,0:T(8,128)(2,1)S(1)} collective-permute-done((bf16[256,640]{1,0:T(8,128)(2,1)}, bf16[256,640]{1,0:T(8,128)(2,1)S(1)}, u32[]{:S(2)}, u32[]{:S(2)}) %collective-permute-start) | collective-permute-done | bytes 327712 | tf_op jit(solution)/shard_map/ppermute | solution.py:597
  104.9 0.0 copy-done
  105.0 17.1 %shard_map.87 = bf16[64,5120]{1,0:T(8,128)(2,1)S(1)} custom-call(bf16[256,640]{1,0:T(8,128)(2,1)S(1)} %collective-permute-done.compact_ref, s32[128]{0:T(128)S(1)} %bitcast.7), custom_call_target="tpu_custom_call" | custom-call | tf_op jit(solution)/shard_map/pallas_call | solution.py:574
  122.1 0.8 copy.15
Async XLA Ops:
  90.6 14.3 %collective-permute-start = (bf16[256,640]{1,0:T(8,128)(2,1)}, bf16[256,640]{1,0:T(8,128)(2,1)S(1)}, u32[]{:S(2)}, u32[]{:S(2)}) collective-permute-start(bf16[256,640]{1,0:T(8,128)(2,1)} %get-tuple-element.7), channel_id=1, source_target_pairs={{16,0},{32,16},{48,32},{64,48},{80,64},{96,80},{112,96},{17,1},{33... | collective-permute-start | bytes 983048 | tf_op jit(solution)/shard_map/ppermute | solution.py:597
  93.3 11.7 %copy-start = (s32[128,1]{0,1:T(1,128)S(1)}, s32[128,1]{0,1:T(1,128)}, u32[]{:S(2)}) copy-start(s32[128,1]{0,1:T(1,128)} %param.12) | copy-start | bytes 1540

commit v2 on v0

v2 whole, which is shorter than its diff:
```python
import jax
import jax.numpy as jnp
from jax import lax
from jax.experimental import pallas as pl
from jax.experimental.pallas import tpu as pltpu
from jax.sharding import PartitionSpec as P

MESH = pl.DeviceIdType.MESH
F32 = jnp.float32
BF16 = jnp.bfloat16
MB = 16
MB_TOK = 32
ROWS = 512
TOKS = (256, 256)
FROM = (0, 256)
D = 5120
CHIP = 640
LOCAL = 320
PART = 160
CHIPS = 8
SLOT = 2 * MB_TOK
PIECE = 48
HEAD, TAIL = (0, PART), (PART, PART)
FIRST, BUT_FIRST = (0, PIECE), (PIECE, LOCAL - PIECE)
LAST, BUT_LAST = (LOCAL - PIECE, PIECE), (0, LOCAL - PIECE)
GU = 1280
MIB = 2**20

MATES = [(0, 1), (0, 2), (0, 3), (1, 0), (1, 1), (1, 2), (1, 3)]
SUM_ORDER = [(1, 2), (1, 1), (1, 3), (0, 1), (0, 3), (0, 2), (1, 0), (0, 0)]
LAG = 3
N_AG = 21
N_RS = 12


def nn_dot(a, b):
    return jnp.dot(a, b, preferred_element_type=F32)


def nt_dot(a, b):
    return lax.dot_general(a, b, (((1,), (1,)), ((), ())), preferred_element_type=F32)


def tn_dot(a, b):
    return lax.dot_general(a, b, (((0,), (0,)), ((), ())), preferred_element_type=F32)


def span(h):
    return slice(FROM[h], FROM[h] + TOKS[h])


def pick(table, k):
    out = table[0]
    for i in range(1, len(table)):
        out = jnp.where(k == i, table[i], out)
    return out


def layer_kernel(
    acts_hbm, grad_hbm, gain_ref, live_ref, senders_ref, wu_hbm, wd_hbm,
    gu_ref, returned_ref,
    wu, wd, g_all, x_all, pre, bh, bp, part, sib_part, r_a, r_b, r_c, r_e, r_d, r_p,
    acts, grads, normed, facts, my_facts, sib_facts, sums, sib_sums, all_sums, weight_rows,
    out_buf, moved, chosen, routed, stage, landed,
    ag_send, ag_recv, facts_send, facts_recv, sums_send, sums_recv,
    sib_send, sib_recv, rs_send, rs_recv, move_send, move_recv, put_send, put_recv,
    local_sem,
):
    s, p = lax.axis_index("section"), lax.axis_index("peer")
    q_me, c = p // 2, p % 2
    z, y, oc = q_me // 4, q_me % 4, 1 - c
    z2, yp, ym, y2 = 1 - z, (y + 1) % 4, (y + 3) % 4, (y + 2) % 4
    sections = lax.axis_size("section")

    def dev(zz, yy, cc):
        return (s, (zz * 4 + yy) * 2 + cc)

    def mate(i):
        dz, dy = MATES[i]
        return dev((z + dz) % 2, (y + dy) % 4, c)

    def mate_from(i):
        dz, dy = MATES[i]
        return ((z + dz) % 2) * 4 + (y + 4 - dy) % 4

    sibling = dev(z, y, oc)
    sends = []

    def remote(src, dst, ssem, rsem, where):
        return pltpu.make_async_remote_copy(
            src_ref=src, dst_ref=dst, send_sem=ssem, recv_sem=rsem,
            device_id=where, device_id_type=MESH,
        )

    def send(src, dst, ssem, rsem, where):
        copy = remote(src, dst, ssem, rsem, where)
        copy.start()
        sends.append(copy)

    def recv(dst, ssem, rsem):
        remote(dst, dst, ssem, rsem, sibling).wait_recv()

    def rows(at, count):
        return pl.ds(pl.multiple_of(at, 16), count)

    load_grad = pltpu.make_async_copy(grad_hbm, grads, local_sem.at[0])
    load_acts = pltpu.make_async_copy(acts_hbm, acts, local_sem.at[1])
    load_wd = pltpu.make_async_copy(wd_hbm.at[0], wd, local_sem.at[2])
    load_wu = pltpu.make_async_copy(wu_hbm.at[0], wu, local_sem.at[3])
    load_grad.start()
    load_acts.start()
    load_wd.start()
    load_wu.start()

    barrier = pltpu.get_barrier_semaphore()
    pl.semaphore_signal(barrier, inc=1, device_id=sibling, device_id_type=MESH)
    for i in range(7):
        pl.semaphore_signal(barrier, inc=1, device_id=mate(i), device_id_type=MESH)
    for step in (1, sections - 1):
        pl.semaphore_signal(
            barrier, inc=1, device_id=((s + step) % sections, p), device_id_type=MESH
        )
    pl.semaphore_wait(barrier, 10)

    bufs = (g_all, x_all)

    def block(a, h, zz, yy, cc, half=None):
        at = (zz * 4 + yy) * CHIP + cc * LOCAL
        first, count = (0, LOCAL) if half is None else half
        return bufs[a][h].at[rows(at + first, count)]

    def ag_start(a, h, tag, zz, yy, where, half=None):
        ref = block(a, h, zz, yy, c, half)
        send(ref, ref, ag_send.at[2 * a + h, tag], ag_recv.at[2 * a + h, tag], where)

    def ag_wait(a, h, tag, zz, yy, cc, half=None):
        recv(block(a, h, zz, yy, cc, half), ag_send.at[2 * a + h, tag], ag_recv.at[2 * a + h, tag])

    def ag_own(a, h):
        ag_start(a, h, 0, z, y, dev(z2, y, c))
        ag_start(a, h, 1, z, y, dev(z, yp, c))
        ag_start(a, h, 2, z, y, dev(z, ym, c))
        ag_start(a, h, 9, z, y, sibling)

    def ag_second(a, h):
        ag_wait(a, h, 1, z, ym, c)
        ag_start(a, h, 3, z, ym, dev(z, yp, c), HEAD)
        ag_wait(a, h, 2, z, yp, c)
        ag_start(a, h, 4, z, yp, dev(z, ym, c), TAIL)
        ag_wait(a, h, 0, z2, y, c)
        ag_start(a, h, 5, z2, y, dev(z, yp, c), BUT_LAST)
        ag_start(a, h, 6, z2, y, dev(z, ym, c), BUT_FIRST)
        ag_start(a, h, 19, z, yp, dev(z2, y, c), FIRST)
        ag_start(a, h, 20, z, ym, dev(z2, y, c), LAST)
        ag_start(a, h, 10, z, ym, sibling)
        ag_start(a, h, 11, z, yp, sibling)
        ag_start(a, h, 12, z2, y, sibling)

    def ag_third(a, h):
        ag_wait(a, h, 3, z, y2, c, HEAD)
        ag_start(a, h, 7, z, y2, dev(z2, y, c), HEAD)
        ag_wait(a, h, 4, z, y2, c, TAIL)
        ag_start(a, h, 8, z, y2, dev(z2, y, c), TAIL)
        ag_start(a, h, 13, z, y2, sibling, HEAD)
        ag_start(a, h, 14, z, y2, sibling, TAIL)

    def ag_fourth(a, h):
        ag_wait(a, h, 5, z2, ym, c, BUT_LAST)
        ag_wait(a, h, 20, z2, ym, c, LAST)
        ag_start(a, h, 15, z2, ym, sibling)
        ag_wait(a, h, 6, z2, yp, c, BUT_FIRST)
        ag_wait(a, h, 19, z2, yp, c, FIRST)
        ag_start(a, h, 16, z2, yp, sibling)
        ag_wait(a, h, 7, z2, y2, c, HEAD)
        ag_start(a, h, 17, z2, y2, sibling, HEAD)
        ag_wait(a, h, 8, z2, y2, c, TAIL)
        ag_start(a, h, 18, z2, y2, sibling, TAIL)

    def multiply(a, h, pair, first=False):
        at = pair * (2 * CHIP)
        at = pl.ds(pl.multiple_of(at, 2 * CHIP), 2 * CHIP)
        if a == 0:
            total, term = bh, nn_dot(wd[:, at], g_all[h][at])
        else:
            total, term = pre, tn_dot(wu[at], x_all[h][at])
        total[h][...] = term if first else total[h][...] + term

    here, across = z * 2 + y // 2, z2 * 2 + y // 2
    here_2, across_2 = z * 2 + 1 - y // 2, z2 * 2 + 1 - y // 2

    def mul_1(a, h):
        ag_wait(a, h, 9, z, y, oc)
        ag_wait(a, h, 10, z, ym, oc)
        ag_wait(a, h, 11, z, yp, oc)
        multiply(a, h, here, True)

    def mul_2(a, h):
        ag_wait(a, h, 13, z, y2, oc, HEAD)
        ag_wait(a, h, 14, z, y2, oc, TAIL)
        multiply(a, h, here_2)

    def mul_3(a, h):
        ag_wait(a, h, 12, z2, y, oc)
        ag_wait(a, h, 15, z2, ym, oc)
        ag_wait(a, h, 16, z2, yp, oc)
        multiply(a, h, across)
        ag_wait(a, h, 17, z2, y2, oc, HEAD)
        ag_wait(a, h, 18, z2, y2, oc, TAIL)
        multiply(a, h, across_2)

    def put_row(ref, at, row):
        ref[at : at + 1] = row[:, 0:256]
        ref[at + 1 : at + 2, 0 : row.shape[1] - 256] = row[:, 256:]

    def get_row(ref, at, count):
        return jnp.concatenate([ref[at : at + 1], ref[at + 1 : at + 2, 0 : count - 256]], axis=1)

    own = rows(q_me * CHIP + c * LOCAL, LOCAL)
    load_acts.wait()
    values = acts[...].astype(F32)
    mean_here = jnp.mean(values, axis=0, keepdims=True)
    spread = values - mean_here
    put_row(my_facts, 0, mean_here)
    put_row(my_facts, 2, jnp.sum(spread * spread, axis=0, keepdims=True))
    gain_row = gain_ref[...].astype(F32)
    put_row(my_facts, 4, gain_row)
    send(my_facts, sib_facts, facts_send.at[7], facts_recv.at[7], sibling)
    load_grad.wait()
    for h in range(2):
        token = lax.broadcasted_iota(jnp.int32, (LOCAL, TOKS[h]), 1) + FROM[h]
        alive = (token // MB_TOK < live_ref[0]).astype(F32)
        g_all[h][own] = (grads[:, span(h)].astype(F32) * alive).astype(BF16)
    recv(sib_facts, facts_send.at[7], facts_recv.at[7])
    mean_a, mean_b = my_facts[0:2], sib_facts[0:2]
    mean_chip = 0.5 * (mean_a + mean_b)
    apart_a, apart_b = mean_a - mean_chip, mean_b - mean_chip
    facts[q_me, 0:2] = mean_chip
    facts[q_me, 2:4] = (
        my_facts[2:4] + sib_facts[2:4] + LOCAL * (apart_a * apart_a + apart_b * apart_b)
    )
    facts[q_me, 4:6] = jnp.where(c == 0, my_facts[4:6], sib_facts[4:6])
    facts[q_me, 6:8] = jnp.where(c == 0, sib_facts[4:6], my_facts[4:6])
    for i in range(7):
        send(facts.at[q_me], facts.at[q_me], facts_send.at[i], facts_recv.at[i], mate(i))
    ag_own(0, 0)
    ag_own(0, 1)
    across_eye = lax.broadcasted_iota(jnp.int32, (LOCAL, LOCAL), 0) == lax.broadcasted_iota(
        jnp.int32, (LOCAL, LOCAL), 1
    )
    gain_col = jnp.sum(jnp.where(across_eye, gain_row, 0.0), axis=1, keepdims=True)
    for i in range(7):
        recv(facts.at[mate_from(i)], facts_send.at[i], facts_recv.at[i])
    means = [facts[i, 0:2] for i in range(CHIPS)]
    mean_two = sum(means) / CHIPS
    square_two = sum(facts[i, 2:4] for i in range(CHIPS))
    square_two += CHIP * sum((m - mean_two) * (m - mean_two) for m in means)
    rstd_two = lax.rsqrt(square_two / D + 1e-05)
    mean_row = jnp.concatenate([mean_two[0:1], mean_two[1:2]], axis=1)
    rstd_row = jnp.concatenate([rstd_two[0:1], rstd_two[1:2]], axis=1)
    normed[...] = (acts[...].astype(F32) - mean_row) * rstd_row
    x_all[0][own] = (normed[:, span(0)] * gain_col).astype(BF16)
    ag_own(1, 0)
    x_all[1][own] = (normed[:, span(1)] * gain_col).astype(BF16)

    def row_sums(h):
        def tile(i, second):
            at = rows(i * 128, 128)
            u = pre[h][at]
            slope = (
                0.5 * (1.0 + lax.erf(u * 0.7071067811865476))
                + u * jnp.exp(-0.5 * u * u) * 0.3989422804014327
            )
            b = (bh[h][at] * slope).astype(BF16)
            bp[h][at] = b
            return second + jnp.sum(b.astype(F32) * u, axis=0, keepdims=True)

        second = lax.fori_loop(0, CHIP // 128, tile, jnp.zeros((1, TOKS[h]), F32))
        first = nn_dot(weight_rows[...], bp[h][...])
        sums[h][0:1] = first[0:1] + first[1:2]
        sums[h][1:2] = second
        send(sums[h], sib_sums[h], sums_send.at[h, 7], sums_recv.at[h, 7], sibling)

    def spread_sums(h):
        recv(sib_sums[h], sums_send.at[h, 7], sums_recv.at[h, 7])
        all_sums[h][q_me] = sums[h][...] + sib_sums[h][...]
        mine = all_sums[h].at[q_me]
        for i in range(7):
            send(mine, mine, sums_send.at[h, i], sums_recv.at[h, i], mate(i))

    def chip(zz, yy):
        return zz * 4 + yy

    def mine_of(h, q, half=None):
        first, count = (0, LOCAL) if half is None else half
        return part[h].at[rows(q * CHIP + c * LOCAL + first, count)]

    def cut(ref, at):
        return ref.at[pl.ds(*at)]

    q_p, q_m, q_2 = chip(z, yp), chip(z, ym), chip(z, y2)
    q_z, q_zp, q_zm, q_z2 = chip(z2, y), chip(z2, yp), chip(z2, ym), chip(z2, y2)

    def sib_copy(h, q):
        return remote(
            part[h].at[rows(q * CHIP + oc * LOCAL, LOCAL)], sib_part[h].at[q],
            sib_send.at[h, q], sib_recv.at[h, q], sibling,
        )

    def rs_copy(h, tag, src, dst, where):
        return remote(src, dst, rs_send.at[h, tag], rs_recv.at[h, tag], where)

    def rs_start(h, tag, src, dst, where):
        copy = rs_copy(h, tag, src, dst, where)
        copy.start()
        sends.append(copy)

    def rs_wait(h, tag, dst):
        recv(dst, rs_send.at[h, tag], rs_recv.at[h, tag])

    def add(ref, *others):
        total = ref[...].astype(F32)
        for other in others:
            total += other[...].astype(F32)
        ref[...] = total.astype(BF16)

    def rs_first(h):
        def put(tag, q, at, dst, where):
            return lambda: rs_copy(h, tag, mine_of(h, q, at), dst, where)

        across, up, down = dev(z2, y, c), dev(z, yp, c), dev(z, ym, c)
        early = [
            [put(0, q_z2, None, r_a[h], across)],
            [
                put(1, q_zp, BUT_FIRST, cut(r_b[h].at[0], BUT_FIRST), up),
                put(10, q_zp, FIRST, r_p[h].at[0], across),
            ],
            [
                put(2, q_zm, BUT_LAST, cut(r_b[h].at[1], BUT_LAST), down),
                put(11, q_zm, LAST, r_p[h].at[1], across),
            ],
            [put(3, q_p, TAIL, cut(r_e[h].at[0], TAIL), up)],
            [put(4, q_m, HEAD, cut(r_e[h].at[1], HEAD), down)],
        ]

        def chip_at(k):
            dz = pick([t[0] for t in SUM_ORDER], k)
            dy = pick([t[1] for t in SUM_ORDER], k)
            return chip((z + dz) % 2, (y + dy) % 4)

        def product(k):
            q = chip_at(k)
            at = pl.ds(pl.multiple_of(q * CHIP, CHIP), CHIP)
            part[h][at] = nn_dot(wu[at], bp[h][...]).astype(BF16)
            sib_copy(h, q).start()

        def join(k):
            q = chip_at(k)
            sib_copy(h, q).wait_recv()
            add(mine_of(h, q), sib_part[h].at[q])

        @pl.loop(0, LAG)
        def _(k):
            product(k)

        @pl.loop(LAG, CHIPS)
        def _(k):
            product(k)
            join(k - LAG)
            for i, makes in enumerate(early):

                @pl.when(k == LAG + i)
                def _(makes=makes):
                    for make in makes:
                        make().start()

        @pl.loop(CHIPS - LAG, CHIPS)
        def _(k):
            join(k)

        for makes in early:
            sends.extend(make() for make in makes)

    def rs_second(h):
        rs_wait(h, 0, r_a[h])
        add(mine_of(h, q_2), r_a[h])
        rs_start(h, 5, mine_of(h, q_2, HEAD), r_c[h].at[0], dev(z, yp, c))
        rs_start(h, 6, mine_of(h, q_2, TAIL), r_c[h].at[1], dev(z, ym, c))
        rs_wait(h, 1, cut(r_b[h].at[0], BUT_FIRST))
        rs_wait(h, 2, cut(r_b[h].at[1], BUT_LAST))
        add(mine_of(h, q_z, BUT_FIRST), cut(r_b[h].at[0], BUT_FIRST))
        add(mine_of(h, q_z, BUT_LAST), cut(r_b[h].at[1], BUT_LAST))
        rs_start(h, 7, mine_of(h, q_z), r_d[h], dev(z2, y, c))
        rs_wait(h, 10, r_p[h].at[0])
        add(mine_of(h, q_p, FIRST), r_p[h].at[0])
        rs_wait(h, 11, r_p[h].at[1])
        add(mine_of(h, q_m, LAST), r_p[h].at[1])

    def rs_third(h):
        rs_wait(h, 5, r_c[h].at[0])
        add(mine_of(h, q_p, HEAD), r_c[h].at[0])
        rs_start(h, 8, mine_of(h, q_p, HEAD), cut(r_e[h].at[0], HEAD), dev(z, yp, c))
        rs_wait(h, 6, r_c[h].at[1])
        add(mine_of(h, q_m, TAIL), r_c[h].at[1])
        rs_start(h, 9, mine_of(h, q_m, TAIL), cut(r_e[h].at[1], TAIL), dev(z, ym, c))

    def move_copy(h):
        return remote(
            out_buf[h], moved[h].at[rows(c * LOCAL, LOCAL)], move_send.at[h, 0],
            move_recv.at[h, 0], ((s + sections - 1) % sections, p),
        )

    def finish(h):
        for i in range(7):
            recv(all_sums[h].at[mate_from(i)], sums_send.at[h, i], sums_recv.at[h, i])
        totals = sum(all_sums[h][i] for i in range(CHIPS)) / D
        rs_wait(h, 7, r_d[h])
        rs_wait(h, 3, cut(r_e[h].at[0], TAIL))
        rs_wait(h, 4, cut(r_e[h].at[1], HEAD))
        rs_wait(h, 8, cut(r_e[h].at[0], HEAD))
        rs_wait(h, 9, cut(r_e[h].at[1], TAIL))
        summed = (
            mine_of(h, q_me)[...].astype(F32)
            + r_d[h][...].astype(F32)
            + r_e[h][0].astype(F32)
            + r_e[h][1].astype(F32)
        )
        at = span(h)
        back = summed * gain_col - totals[0:1] - normed[:, at] * totals[1:2]
        total = rstd_row[:, at] * back + g_all[h][own].astype(F32)
        out_buf[h][...] = total.astype(BF16)

        @pl.when(s > 0)
        def _():
            move_copy(h).start()

    def move_second(h):
        there = moved[h].at[rows(c * LOCAL, LOCAL)]

        @pl.when(s < sections - 1)
        def _():
            recv(there, move_send.at[h, 0], move_recv.at[h, 0])

        @pl.when(s == sections - 1)
        def _():
            there[...] = jnp.zeros((LOCAL, TOKS[h]), BF16)

        send(there, there, move_send.at[h, 1], move_recv.at[h, 1], sibling)

    def place_rows(h):
        recv(moved[h].at[rows(oc * LOCAL, LOCAL)], move_send.at[h, 1], move_recv.at[h, 1])
        return nt_dot(chosen[:, span(h)], moved[h][...])

    count = live_ref[0].astype(F32)

    def grad_up(k):
        at = pl.ds(k * GU, GU)
        term = nt_dot(x_all[0][at], bp[0][...]) + nt_dot(x_all[1][at], bp[1][...])
        gu_ref[at] = (term / count).astype(BF16)

    ag_second(0, 0)
    load_wd.wait()
    ag_second(1, 0)
    ag_own(1, 1)
    ag_second(0, 1)
    mul_1(0, 0)
    load_wu.wait()
    mul_1(1, 0)
    ag_third(0, 0)
    ag_third(1, 0)
    weights = jnp.zeros((16, CHIP), F32)
    for i in range(CHIPS):
        for j in range(2):
            gain_ij = get_row(facts.at[i], 4 + 2 * j, LOCAL)
            gain_ij = jnp.broadcast_to(gain_ij, (16, LOCAL)).astype(BF16)
            at = i * CHIP + j * LOCAL
            weights += nn_dot(gain_ij, wu[at : at + LOCAL])
    high = weights.astype(BF16).astype(F32)
    line = lax.broadcasted_iota(jnp.int32, (16, CHIP), 0)
    weight_rows[...] = jnp.where(
        line == 0, high, jnp.where(line == 1, weights - high, 0.0)
    ).astype(BF16)
    mul_2(0, 0)
    mul_2(1, 0)
    ag_second(1, 1)
    ag_fourth(0, 0)
    mul_3(0, 0)
    ag_fourth(1, 0)
    ag_third(0, 1)
    mul_3(1, 0)
    row_sums(0)
    rs_first(0)
    spread_sums(0)
    ag_third(1, 1)
    mul_1(0, 1)
    mul_1(1, 1)
    rs_second(0)
    ag_fourth(0, 1)
    mul_2(0, 1)
    mul_2(1, 1)
    mul_3(0, 1)
    rs_third(0)
    ag_fourth(1, 1)
    mul_3(1, 1)
    row_sums(1)
    rs_first(1)
    spread_sums(1)
    finish(0)

    base = jnp.minimum(s + 1, sections - 1) * MB
    names = [senders_ref[base + m] for m in range(MB)]
    token = lax.broadcasted_iota(jnp.int32, (SLOT, ROWS), 1)
    slot_row = token % MB_TOK
    for m in range(MB):
        rank = jnp.int32(0)
        for before in range(m):
            rank = rank + jnp.where(names[before] == names[m], 1, 0)
        slot_row += jnp.where(token // MB_TOK == m, (names[m] * 2 + rank) * MB_TOK, 0)
    row = lax.broadcasted_iota(jnp.int32, (SLOT, ROWS), 0)
    for i, (dz, dy) in enumerate(MATES + [(0, 0)]):
        peer = chip((z + dz) % 2, (y + dy) % 4) * 2 + c
        chosen[i * SLOT : (i + 1) * SLOT] = jnp.where(
            slot_row == row + peer * SLOT, 1.0, 0.0
        ).astype(BF16)

    grad_up(0)
    rs_second(1)
    move_second(0)
    grad_up(1)
    rs_third(1)
    routed[...] = place_rows(0)
    grad_up(2)
    grad_up(3)
    finish(1)
    move_second(1)
    routed[...] += place_rows(1)
    columns = pl.ds(pl.multiple_of(q_me * CHIP, CHIP), CHIP)
    for i in range(7):
        stage[i] = routed[i * SLOT : (i + 1) * SLOT].astype(BF16)
        send(stage.at[i], landed.at[:, columns], put_send.at[i], put_recv.at[i], mate(i))
    landed[:, columns] = routed[7 * SLOT :].astype(BF16)
    for i in range(7):
        there = landed.at[:, pl.ds(pl.multiple_of(mate_from(i) * CHIP, CHIP), CHIP)]
        recv(there, put_send.at[i], put_recv.at[i])
    returned_ref[...] = landed[...]

    for h in range(2):

        @pl.loop(0, CHIPS)
        def _(k):
            sib_copy(h, k).wait_send()

        @pl.when(s > 0)
        def _():
            move_copy(h).wait_send()

    for copy in sends:
        copy.wait_send()


def both(make):
    return tuple(make(t) for t in TOKS)


def layer(acts, grad_out, gain, live, senders, w_up, w_down):
    vmem, anyspace = pl.BlockSpec(memory_space=pltpu.VMEM), pl.BlockSpec(memory_space=pl.ANY)
    smem = pl.BlockSpec(memory_space=pltpu.SMEM)
    dma = pltpu.SemaphoreType.DMA
    return pl.pallas_call(
        layer_kernel,
        out_shape=[
            pltpu.VMEM((D, CHIP), BF16),
            pltpu.VMEM((SLOT, D), BF16),
        ],
        in_specs=[anyspace, anyspace, vmem, smem, smem, anyspace, anyspace],
        out_specs=[vmem, vmem],
        scratch_shapes=[
            pltpu.VMEM((D, CHIP), BF16),
            pltpu.VMEM((CHIP, D), BF16),
            both(lambda t: pltpu.VMEM((D, t), BF16)),
            both(lambda t: pltpu.VMEM((D, t), BF16)),
            both(lambda t: pltpu.VMEM((CHIP, t), F32)),
            both(lambda t: pltpu.VMEM((CHIP, t), F32)),
            both(lambda t: pltpu.VMEM((CHIP, t), BF16)),
            both(lambda t: pltpu.VMEM((D, t), BF16)),
            both(lambda t: pltpu.VMEM((CHIPS, LOCAL, t), BF16)),
            both(lambda t: pltpu.VMEM((LOCAL, t), BF16)),
            both(lambda t: pltpu.VMEM((2, LOCAL, t), BF16)),
            both(lambda t: pltpu.VMEM((2, PART, t), BF16)),
            both(lambda t: pltpu.VMEM((2, LOCAL, t), BF16)),
            both(lambda t: pltpu.VMEM((LOCAL, t), BF16)),
            both(lambda t: pltpu.VMEM((2, PIECE, t), BF16)),
            pltpu.VMEM((LOCAL, ROWS), BF16),
            pltpu.VMEM((LOCAL, ROWS), BF16),
            pltpu.VMEM((LOCAL, ROWS), F32),
            pltpu.VMEM((CHIPS, 8, 256), F32),
            pltpu.VMEM((8, 256), F32),
            pltpu.VMEM((8, 256), F32),
            both(lambda t: pltpu.VMEM((8, t), F32)),
            both(lambda t: pltpu.VMEM((8, t), F32)),
            both(lambda t: pltpu.VMEM((CHIPS, 8, t), F32)),
            pltpu.VMEM((16, CHIP), BF16),
            both(lambda t: pltpu.VMEM((LOCAL, t), BF16)),
            both(lambda t: pltpu.VMEM((CHIP, t), BF16)),
            pltpu.VMEM((CHIPS * SLOT, ROWS), BF16),
            pltpu.VMEM((CHIPS * SLOT, CHIP), F32),
            pltpu.VMEM((7, SLOT, CHIP), BF16),
            pltpu.VMEM((SLOT, D), BF16),
            dma((4, N_AG)),
            dma((4, N_AG)),
            dma((8,)),
            dma((8,)),
            dma((2, 8)),
            dma((2, 8)),
            dma((2, CHIPS)),
            dma((2, CHIPS)),
            dma((2, N_RS)),
            dma((2, N_RS)),
            dma((2, 2)),
            dma((2, 2)),
            dma((7,)),
            dma((7,)),
            dma((4,)),
        ],
        compiler_params=pltpu.CompilerParams(
            collective_id=0, has_side_effects=True, vmem_limit_bytes=48 * MIB
        ),
        cost_estimate=pl.CostEstimate(
            flops=8 * ROWS * D * CHIP, bytes_accessed=20 * MIB, transcendentals=2 * ROWS * CHIP
        ),
    )(acts, grad_out, gain, live, senders, w_up, w_down)


def body(acts, grad_out, gain, w_up, w_down, senders, live):
    grad_up, returned = layer(acts.T, grad_out.T, gain, live, senders[:, 0], w_up, w_down)
    return (grad_up[None], returned)


def solution(mesh):
    in_specs = (
        P("section", "peer"),
        P("section", "peer"),
        P("section", "peer"),
        P("section", None, "peer"),
        P("section", "peer", None),
        P(),
        P("section"),
    )
    out_specs = (P("section", None, "peer"), P(("section", "peer"), None))
    return jax.shard_map(body, mesh=mesh, in_specs=in_specs, out_specs=out_specs, check_vma=False)
```

time: 247 us -> 103 us (0.42); the launches traced: 243 us -> 102 us
  Pallas kernels: 0 us -> 97 us
  waiting for transfers between devices: 74.2 us -> 0 us
  blocking collectives: 53.5 us -> 0 us
  matrix products: 39 us -> 0 us
  local copies, waits for them, and re-layouts: 35.1 us -> 3.63 us
  other arithmetic: 22.8 us -> 0 us
  between operations: 15.3 us -> 1.29 us
  starting transfers between devices: 2.73 us -> 0 us
    pallas_call x0 -> x1, Pallas kernels: none -> 97 us  [layer(): pl.pallas_call(layer_kernel, out_shape=[pltpu.VMEM((D, CHIP), BF16), pltp...]
    reduce_scatter x1 -> x0, waiting for transfers between devices: 55.7 us -> none  [body(): lax.psum_scatter((lax.dot_general(piece, up_local, (((1,), (1,)), ((), ()...]
    unnamed x1 -> x0, blocking collectives: 53.5 us -> none
    dot_general x4 -> x0, matrix products: 39 us -> none  [the longest x1 14.1 us: body(): lax.dot_general(piece, up_local, (((1,), (1,)), ((), ())), preferred_elem...]
    all_gather x2 -> x0, local copies, waits for them, and re-layouts: 15.9 us -> none  [the longest x1 8.01 us: body(): lax.all_gather(acts, 'peer', axis=1, tiled=True)]
    gather x4 -> x0, local copies, waits for them, and re-layouts: 15.3 us -> none  [the longest x1 5.78 us: body(): jnp.take(normed, picked, axis=0)]
    all_gather x2 -> x0, waiting for transfers between devices: 11.8 us -> none  [the longest x1 11.8 us: body(): lax.all_gather(grad_out, 'peer', axis=1, tiled=True)]
    mul x3 -> x0, other arithmetic: 8.26 us -> none  [the longest x1 8.25 us: body(): normed = centre * rstd]
  transfers between devices with their start and end apart: 4 -> 0, of which waited for: 3 -> 0; matrix products, arithmetic and copies ran while one was open for 19% -> 0% of each run, Pallas kernels for 0% -> 0%
where the time goes in v2:
time: 103 us; the launch traced here: 102 us
  Pallas kernels  97 us (94%)
  local copies, waits for them, and re-layouts  3.63 us (4%)
  between operations  1.29 us (1%)
    pallas_call x1, Pallas kernels, layer(): pl.pallas_call(layer_kernel, out_shape=[pltpu.VMEM((D, CHIP), BF16), pltp...  97 us
    unnamed x2, local copies, waits for them, and re-layouts  3.63 us

profile of v2, /device:TPU:7, one launch (start us, length us, event | category | flops | bytes accessed | tf_op | source)
XLA Modules:
  0.0 102.0 jit_solution(499991648958050204)
XLA Ops:
  1.3 97.0 %shard_map.86 = (bf16[5120,640]{1,0:T(8,128)(2,1)S(1)}, bf16[64,5120]{1,0:T(8,128)(2,1)S(1)}) custom-call(bf16[320,512]{1,0:T(8,128)(2,1)} %bitcast.5, bf16[320,512]{1,0:T(8,128)(2,1)} %bitcast.6, bf16[1,320]{1,0:T(2,128)(2,1)} %gain_ref.1, s32[1]{0:T(128)S(6)} %copy.13.live_ref, s32[128]{0:T(128)} %bitcast.7, bf16[1,5120,640]{2,1,0:T(8,128)(2,1)} %wu_hbm.1, ...), custom_call_target="tpu_custom_call" | custom-call | flops 13421772800 | bytes 20971520 | tf_op jit(solution)/shard_map/pallas_call | solution.py:568
  98.3 2.8 %copy.11 = bf16[1,5120,640]{2,1,0:T(8,128)(2,1)} copy(bf16[1,5120,640]{2,1,0:T(8,128)(2,1)S(1)} %bitcast.4) | data formatting | bytes 13107200
  101.1 0.8 copy.12

commit v3 on v2

--- a/solution.py
+++ b/solution.py
@@ -23,6 +23,8 @@
 HEAD, TAIL = (0, PART), (PART, PART)
 FIRST, BUT_FIRST = (0, PIECE), (PIECE, LOCAL - PIECE)
 LAST, BUT_LAST = (LOCAL - PIECE, PIECE), (0, LOCAL - PIECE)
+PARTS = (((LOCAL, PIECE),), ((LOCAL, PIECE),))
+WIDTHS = (128, 128, 64)
 GU = 1280
 MIB = 2**20
 
@@ -61,7 +63,7 @@
     gu_ref, returned_ref,
     wu, wd, g_all, x_all, pre, bh, bp, part, sib_part, r_a, r_b, r_c, r_e, r_d, r_p,
     acts, grads, normed, facts, my_facts, sib_facts, sums, sib_sums, all_sums, weight_rows,
-    out_buf, moved, chosen, routed, stage, landed,
+    gain_rows, out_buf, moved, chosen, routed, stage, landed,
     ag_send, ag_recv, facts_send, facts_recv, sums_send, sums_recv,
     sib_send, sib_recv, rs_send, rs_recv, move_send, move_recv, put_send, put_recv,
     local_sem,
@@ -142,18 +144,20 @@
         ag_start(a, h, 2, z, y, dev(z, ym, c))
         ag_start(a, h, 9, z, y, sibling)
 
-    def ag_second(a, h):
+    def ag_halves(a, h):
         ag_wait(a, h, 1, z, ym, c)
         ag_start(a, h, 3, z, ym, dev(z, yp, c), HEAD)
         ag_wait(a, h, 2, z, yp, c)
         ag_start(a, h, 4, z, yp, dev(z, ym, c), TAIL)
-        ag_wait(a, h, 0, z2, y, c)
-        ag_start(a, h, 5, z2, y, dev(z, yp, c), BUT_LAST)
-        ag_start(a, h, 6, z2, y, dev(z, ym, c), BUT_FIRST)
         ag_start(a, h, 19, z, yp, dev(z2, y, c), FIRST)
         ag_start(a, h, 20, z, ym, dev(z2, y, c), LAST)
         ag_start(a, h, 10, z, ym, sibling)
         ag_start(a, h, 11, z, yp, sibling)
+
+    def ag_across(a, h):
+        ag_wait(a, h, 0, z2, y, c)
+        ag_start(a, h, 5, z2, y, dev(z, yp, c), BUT_LAST)
+        ag_start(a, h, 6, z2, y, dev(z, ym, c), BUT_FIRST)
         ag_start(a, h, 12, z2, y, sibling)
 
     def ag_third(a, h):
@@ -216,6 +220,12 @@
         return jnp.concatenate([ref[at : at + 1], ref[at + 1 : at + 2, 0 : count - 256]], axis=1)
 
     own = rows(q_me * CHIP + c * LOCAL, LOCAL)
+    load_grad.wait()
+    for h in range(2):
+        token = lax.broadcasted_iota(jnp.int32, (LOCAL, TOKS[h]), 1) + FROM[h]
+        alive = (token // MB_TOK < live_ref[0]).astype(F32)
+        g_all[h][own] = (grads[:, span(h)].astype(F32) * alive).astype(BF16)
+    ag_own(0, 0)
     load_acts.wait()
     values = acts[...].astype(F32)
     mean_here = jnp.mean(values, axis=0, keepdims=True)
@@ -225,11 +235,6 @@
     gain_row = gain_ref[...].astype(F32)
     put_row(my_facts, 4, gain_row)
     send(my_facts, sib_facts, facts_send.at[7], facts_recv.at[7], sibling)
-    load_grad.wait()
-    for h in range(2):
-        token = lax.broadcasted_iota(jnp.int32, (LOCAL, TOKS[h]), 1) + FROM[h]
-        alive = (token // MB_TOK < live_ref[0]).astype(F32)
-        g_all[h][own] = (grads[:, span(h)].astype(F32) * alive).astype(BF16)
     recv(sib_facts, facts_send.at[7], facts_recv.at[7])
     mean_a, mean_b = my_facts[0:2], sib_facts[0:2]
     mean_chip = 0.5 * (mean_a + mean_b)
@@ -242,12 +247,12 @@
     facts[q_me, 6:8] = jnp.where(c == 0, sib_facts[4:6], my_facts[4:6])
     for i in range(7):
         send(facts.at[q_me], facts.at[q_me], facts_send.at[i], facts_recv.at[i], mate(i))
-    ag_own(0, 0)
     ag_own(0, 1)
     across_eye = lax.broadcasted_iota(jnp.int32, (LOCAL, LOCAL), 0) == lax.broadcasted_iota(
         jnp.int32, (LOCAL, LOCAL), 1
     )
     gain_col = jnp.sum(jnp.where(across_eye, gain_row, 0.0), axis=1, keepdims=True)
+    gain_rows[...] = jnp.broadcast_to(gain_col, (LOCAL, 128))
     for i in range(7):
         recv(facts.at[mate_from(i)], facts_send.at[i], facts_recv.at[i])
     means = [facts[i, 0:2] for i in range(CHIPS)]
@@ -258,9 +263,9 @@
     mean_row = jnp.concatenate([mean_two[0:1], mean_two[1:2]], axis=1)
     rstd_row = jnp.concatenate([rstd_two[0:1], rstd_two[1:2]], axis=1)
     normed[...] = (acts[...].astype(F32) - mean_row) * rstd_row
-    x_all[0][own] = (normed[:, span(0)] * gain_col).astype(BF16)
-    ag_own(1, 0)
-    x_all[1][own] = (normed[:, span(1)] * gain_col).astype(BF16)
+    for h in range(2):
+        x_all[h][own] = (normed[:, span(h)] * gain_col).astype(BF16)
+        ag_own(1, h)
 
     def row_sums(h):
         def tile(i, second):
@@ -290,12 +295,30 @@
     def chip(zz, yy):
         return zz * 4 + yy
 
-    def mine_of(h, q, half=None):
-        first, count = (0, LOCAL) if half is None else half
+    def offset(j):
+        return (c * 192, 128 - c * 64, (1 - c) * 256)[j]
+
+    def part_rows(h, j):
+        count, over = PARTS[h][j]
+        first = offset(j) if len(PARTS[h]) > 1 else 0
+        half = count // 2
+        return dict(
+            all=(first, count),
+            head=(first, half),
+            tail=(first + half, half),
+            first=(first, over),
+            but_first=(first + over, count - over),
+            last=(first + count - over, over),
+            but_last=(first, count - over),
+        )
+
+    def mine_of(h, q, at):
+        first, count = at
         return part[h].at[rows(q * CHIP + c * LOCAL + first, count)]
 
     def cut(ref, at):
-        return ref.at[pl.ds(*at)]
+        first, count = at
+        return ref.at[rows(first, count)]
 
     q_p, q_m, q_2 = chip(z, yp), chip(z, ym), chip(z, y2)
     q_z, q_zp, q_zm, q_z2 = chip(z2, y), chip(z2, yp), chip(z2, ym), chip(z2, y2)
@@ -307,7 +330,7 @@
         )
 
     def rs_copy(h, tag, src, dst, where):
-        return remote(src, dst, rs_send.at[h, tag], rs_recv.at[h, tag], where)
+        return remote(src, dst, rs_send.at[tag], rs_recv.at[tag], where)
 
     def rs_start(h, tag, src, dst, where):
         copy = rs_copy(h, tag, src, dst, where)
@@ -315,7 +338,7 @@
         sends.append(copy)
 
     def rs_wait(h, tag, dst):
-        recv(dst, rs_send.at[h, tag], rs_recv.at[h, tag])
+        recv(dst, rs_send.at[tag], rs_recv.at[tag])
 
     def add(ref, *others):
         total = ref[...].astype(F32)
@@ -323,24 +346,33 @@
             total += other[...].astype(F32)
         ref[...] = total.astype(BF16)
 
+    def tags(h, j):
+        return (h * len(PARTS[0]) + j) * N_RS
+
     def rs_first(h):
-        def put(tag, q, at, dst, where):
-            return lambda: rs_copy(h, tag, mine_of(h, q, at), dst, where)
-
         across, up, down = dev(z2, y, c), dev(z, yp, c), dev(z, ym, c)
-        early = [
-            [put(0, q_z2, None, r_a[h], across)],
-            [
-                put(1, q_zp, BUT_FIRST, cut(r_b[h].at[0], BUT_FIRST), up),
-                put(10, q_zp, FIRST, r_p[h].at[0], across),
-            ],
-            [
-                put(2, q_zm, BUT_LAST, cut(r_b[h].at[1], BUT_LAST), down),
-                put(11, q_zm, LAST, r_p[h].at[1], across),
-            ],
-            [put(3, q_p, TAIL, cut(r_e[h].at[0], TAIL), up)],
-            [put(4, q_m, HEAD, cut(r_e[h].at[1], HEAD), down)],
-        ]
+
+        def puts(j):
+            t, at = tags(h, j), part_rows(h, j)
+
+            def put(tag, q, where, dst, to):
+                return lambda: rs_copy(h, t + tag, mine_of(h, q, at[where]), cut(dst, at[where]), to)
+
+            return [
+                [put(0, q_z2, "all", r_a[h], across)],
+                [
+                    put(1, q_zp, "but_first", r_b[h].at[0], up),
+                    put(10, q_zp, "first", r_p[h].at[0], across),
+                ],
+                [
+                    put(2, q_zm, "but_last", r_b[h].at[1], down),
+                    put(11, q_zm, "last", r_p[h].at[1], across),
+                ],
+                [put(3, q_p, "tail", r_e[h].at[0], up)],
+                [put(4, q_m, "head", r_e[h].at[1], down)],
+            ]
+
+        early = [puts(j) for j in range(len(PARTS[h]))]
 
         def chip_at(k):
             dz = pick([t[0] for t in SUM_ORDER], k)
@@ -356,7 +388,7 @@
         def join(k):
             q = chip_at(k)
             sib_copy(h, q).wait_recv()
-            add(mine_of(h, q), sib_part[h].at[q])
+            add(mine_of(h, q, (0, LOCAL)), sib_part[h].at[q])
 
         @pl.loop(0, LAG)
         def _(k):
@@ -366,7 +398,7 @@
         def _(k):
             product(k)
             join(k - LAG)
-            for i, makes in enumerate(early):
+            for i, makes in enumerate(early[0]):
 
                 @pl.when(k == LAG + i)
                 def _(makes=makes):
@@ -377,78 +409,124 @@
         def _(k):
             join(k)
 
-        for makes in early:
-            sends.extend(make() for make in makes)
-
-    def rs_second(h):
-        rs_wait(h, 0, r_a[h])
-        add(mine_of(h, q_2), r_a[h])
-        rs_start(h, 5, mine_of(h, q_2, HEAD), r_c[h].at[0], dev(z, yp, c))
-        rs_start(h, 6, mine_of(h, q_2, TAIL), r_c[h].at[1], dev(z, ym, c))
-        rs_wait(h, 1, cut(r_b[h].at[0], BUT_FIRST))
-        rs_wait(h, 2, cut(r_b[h].at[1], BUT_LAST))
-        add(mine_of(h, q_z, BUT_FIRST), cut(r_b[h].at[0], BUT_FIRST))
-        add(mine_of(h, q_z, BUT_LAST), cut(r_b[h].at[1], BUT_LAST))
-        rs_start(h, 7, mine_of(h, q_z), r_d[h], dev(z2, y, c))
-        rs_wait(h, 10, r_p[h].at[0])
-        add(mine_of(h, q_p, FIRST), r_p[h].at[0])
-        rs_wait(h, 11, r_p[h].at[1])
-        add(mine_of(h, q_m, LAST), r_p[h].at[1])
-
-    def rs_third(h):
-        rs_wait(h, 5, r_c[h].at[0])
-        add(mine_of(h, q_p, HEAD), r_c[h].at[0])
-        rs_start(h, 8, mine_of(h, q_p, HEAD), cut(r_e[h].at[0], HEAD), dev(z, yp, c))
-        rs_wait(h, 6, r_c[h].at[1])
-        add(mine_of(h, q_m, TAIL), r_c[h].at[1])
-        rs_start(h, 9, mine_of(h, q_m, TAIL), cut(r_e[h].at[1], TAIL), dev(z, ym, c))
-
-    def move_copy(h):
+        for j, groups in enumerate(early):
+            for make in [m for group in groups for m in group]:
+                copy = make()
+                if j > 0:
+                    copy.start()
+                sends.append(copy)
+
+    def rs_second(h, j=0):
+        t, at = tags(h, j), part_rows(h, j)
+        rs_wait(h, t, cut(r_a[h], at["all"]))
+        add(mine_of(h, q_2, at["all"]), cut(r_a[h], at["all"]))
+        head, tail = at["head"], at["tail"]
+        rs_start(h, t + 5, mine_of(h, q_2, head), cut(r_c[h].at[0], head), dev(z, yp, c))
+        rs_start(h, t + 6, mine_of(h, q_2, tail), cut(r_c[h].at[1], tail), dev(z, ym, c))
+        from_m, from_p = cut(r_b[h].at[0], at["but_first"]), cut(r_b[h].at[1], at["but_last"])
+        rs_wait(h, t + 1, from_m)
+        rs_wait(h, t + 2, from_p)
+        add(mine_of(h, q_z, at["but_first"]), from_m)
+        add(mine_of(h, q_z, at["but_last"]), from_p)
+        rs_start(
+            h, t + 7, mine_of(h, q_z, at["all"]), cut(r_d[h], at["all"]), dev(z2, y, c)
+        )
+        for tag, q, i, where in ((10, q_p, 0, "first"), (11, q_m, 1, "last")):
+            there = cut(r_p[h].at[i], at[where])
+            rs_wait(h, t + tag, there)
+            add(mine_of(h, q, at[where]), there)
+
+    def rs_third(h, j=0):
+        t, at = tags(h, j), part_rows(h, j)
+        for tag, q, i, where, to in (
+            (0, q_p, 0, "head", dev(z, yp, c)),
+            (1, q_m, 1, "tail", dev(z, ym, c)),
+        ):
+            there = cut(r_c[h].at[i], at[where])
+            rs_wait(h, t + 5 + tag, there)
+            add(mine_of(h, q, at[where]), there)
+            rs_start(h, t + 8 + tag, mine_of(h, q, at[where]), cut(r_e[h].at[i], at[where]), to)
+
+    starts = [2 * sum(WIDTHS[:j]) for j in range(3)]
+
+    def place_of(h, j, core):
+        return moved[h].at[rows(starts[j] + core * WIDTHS[j], WIDTHS[j])]
+
+    def move_copy(h, j):
         return remote(
-            out_buf[h], moved[h].at[rows(c * LOCAL, LOCAL)], move_send.at[h, 0],
-            move_recv.at[h, 0], ((s + sections - 1) % sections, p),
+            out_buf[h].at[rows(offset(j), WIDTHS[j])], place_of(h, j, c), move_send.at[h, j],
+            move_recv.at[h, j], ((s + sections - 1) % sections, p),
         )
 
-    def finish(h):
+    def totals_of(h):
         for i in range(7):
             recv(all_sums[h].at[mate_from(i)], sums_send.at[h, i], sums_recv.at[h, i])
-        totals = sum(all_sums[h][i] for i in range(CHIPS)) / D
-        rs_wait(h, 7, r_d[h])
-        rs_wait(h, 3, cut(r_e[h].at[0], TAIL))
-        rs_wait(h, 4, cut(r_e[h].at[1], HEAD))
-        rs_wait(h, 8, cut(r_e[h].at[0], HEAD))
-        rs_wait(h, 9, cut(r_e[h].at[1], TAIL))
-        summed = (
-            mine_of(h, q_me)[...].astype(F32)
-            + r_d[h][...].astype(F32)
-            + r_e[h][0].astype(F32)
-            + r_e[h][1].astype(F32)
-        )
-        at = span(h)
-        back = summed * gain_col - totals[0:1] - normed[:, at] * totals[1:2]
-        total = rstd_row[:, at] * back + g_all[h][own].astype(F32)
-        out_buf[h][...] = total.astype(BF16)
+        return sum(all_sums[h][i] for i in range(CHIPS)) / D
+
+    def finish(h, totals, j=0):
+        t, at = tags(h, j), part_rows(h, j)
+        mine = at["all"]
+        rs_wait(h, t + 7, cut(r_d[h], mine))
+        rs_wait(h, t + 3, cut(r_e[h].at[0], at["tail"]))
+        rs_wait(h, t + 4, cut(r_e[h].at[1], at["head"]))
+        rs_wait(h, t + 8, cut(r_e[h].at[0], at["head"]))
+        rs_wait(h, t + 9, cut(r_e[h].at[1], at["tail"]))
+        summed = mine_of(h, q_me, mine)[...].astype(F32)
+        for ref in (r_d[h], r_e[h].at[0], r_e[h].at[1]):
+            summed += cut(ref, mine)[...].astype(F32)
+        here = rows(*mine)
+        gain_here = gain_rows[here, 0:1]
+        back = summed * gain_here - totals[0:1] - normed[here, span(h)] * totals[1:2]
+        grad_here = g_all[h][rows(q_me * CHIP + c * LOCAL + mine[0], mine[1])].astype(F32)
+        out_buf[h][here] = (rstd_row[:, span(h)] * back + grad_here).astype(BF16)
 
         @pl.when(s > 0)
         def _():
-            move_copy(h).start()
-
-    def move_second(h):
-        there = moved[h].at[rows(c * LOCAL, LOCAL)]
+            for i in range(3) if len(PARTS[h]) == 1 else (j,):
+                move_copy(h, i).start()
+
+    def move_second(h, j):
+        there = place_of(h, j, c)
 
         @pl.when(s < sections - 1)
         def _():
-            recv(there, move_send.at[h, 0], move_recv.at[h, 0])
+            recv(there, move_send.at[h, j], move_recv.at[h, j])
 
         @pl.when(s == sections - 1)
         def _():
-            there[...] = jnp.zeros((LOCAL, TOKS[h]), BF16)
-
-        send(there, there, move_send.at[h, 1], move_recv.at[h, 1], sibling)
-
-    def place_rows(h):
-        recv(moved[h].at[rows(oc * LOCAL, LOCAL)], move_send.at[h, 1], move_recv.at[h, 1])
-        return nt_dot(chosen[:, span(h)], moved[h][...])
+            there[...] = jnp.zeros((WIDTHS[j], TOKS[h]), BF16)
+
+        send(there, there, move_send.at[h, 3 + j], move_recv.at[h, 3 + j], sibling)
+
+    def place_rows(h, j):
+        recv(place_of(h, j, oc), move_send.at[h, 3 + j], move_recv.at[h, 3 + j])
+        features = moved[h][starts[j] : starts[j] + 2 * WIDTHS[j]]
+        return nt_dot(chosen[:, span(h)], features)
+
+    COLUMNS = (((0, 128, 0), (512, 128, 128)), ((128, 128, 0), (384, 128, 128)), ((256, 128, 0),))
+
+    def part_columns(q, at, width):
+        return pl.ds(pl.multiple_of(q * CHIP + at, 128), width)
+
+    def put_part(j):
+        width = 2 * WIDTHS[j]
+        both_phases = routed[:, starts[j] : starts[j] + width] + place_rows(1, j)
+        stage[j][...] = both_phases.astype(BF16)
+        for i in range(7):
+            for n, (at, size, source) in enumerate(COLUMNS[j]):
+                send(
+                    stage[j].at[pl.ds(i * SLOT, SLOT), pl.ds(source, size)],
+                    landed.at[:, part_columns(q_me, at, size)],
+                    put_send.at[i, 2 * j + n], put_recv.at[i, 2 * j + n], mate(i),
+                )
+        for at, size, source in COLUMNS[j]:
+            landed[:, part_columns(q_me, at, size)] = stage[j][7 * SLOT :, source : source + size]
+
+    def wait_part(j):
+        for i in range(7):
+            for n, (at, size, _) in enumerate(COLUMNS[j]):
+                there = landed.at[:, part_columns(mate_from(i), at, size)]
+                recv(there, put_send.at[i, 2 * j + n], put_recv.at[i, 2 * j + n])
 
     count = live_ref[0].astype(F32)
 
@@ -457,16 +535,8 @@
         term = nt_dot(x_all[0][at], bp[0][...]) + nt_dot(x_all[1][at], bp[1][...])
         gu_ref[at] = (term / count).astype(BF16)
 
-    ag_second(0, 0)
-    load_wd.wait()
-    ag_second(1, 0)
-    ag_own(1, 1)
-    ag_second(0, 1)
-    mul_1(0, 0)
+    ag_halves(0, 0)
     load_wu.wait()
-    mul_1(1, 0)
-    ag_third(0, 0)
-    ag_third(1, 0)
     weights = jnp.zeros((16, CHIP), F32)
     for i in range(CHIPS):
         for j in range(2):
@@ -479,33 +549,6 @@
     weight_rows[...] = jnp.where(
         line == 0, high, jnp.where(line == 1, weights - high, 0.0)
     ).astype(BF16)
-    mul_2(0, 0)
-    mul_2(1, 0)
-    ag_second(1, 1)
-    ag_fourth(0, 0)
-    mul_3(0, 0)
-    ag_fourth(1, 0)
-    ag_third(0, 1)
-    mul_3(1, 0)
-    row_sums(0)
-    rs_first(0)
-    spread_sums(0)
-    ag_third(1, 1)
-    mul_1(0, 1)
-    mul_1(1, 1)
-    rs_second(0)
-    ag_fourth(0, 1)
-    mul_2(0, 1)
-    mul_2(1, 1)
-    mul_3(0, 1)
-    rs_third(0)
-    ag_fourth(1, 1)
-    mul_3(1, 1)
-    row_sums(1)
-    rs_first(1)
-    spread_sums(1)
-    finish(0)
-
     base = jnp.minimum(s + 1, sections - 1) * MB
     names = [senders_ref[base + m] for m in range(MB)]
     token = lax.broadcasted_iota(jnp.int32, (SLOT, ROWS), 1)
@@ -522,25 +565,62 @@
             slot_row == row + peer * SLOT, 1.0, 0.0
         ).astype(BF16)
 
-    grad_up(0)
+    load_wd.wait()
+    mul_1(0, 0)
+    ag_halves(1, 0)
+    ag_across(0, 0)
+    ag_across(1, 0)
+    ag_halves(0, 1)
+    ag_halves(1, 1)
+    ag_across(0, 1)
+    ag_across(1, 1)
+    mul_1(1, 0)
+    mul_1(0, 1)
+    ag_third(0, 0)
+    mul_1(1, 1)
+    ag_third(1, 0)
+    mul_2(0, 0)
+    mul_2(1, 0)
+    ag_fourth(0, 0)
+    mul_3(0, 0)
+    ag_fourth(1, 0)
+    ag_third(0, 1)
+    mul_3(1, 0)
+    row_sums(0)
+    ag_third(1, 1)
+    rs_first(0)
+    spread_sums(0)
+    mul_2(0, 1)
+    ag_fourth(0, 1)
+    mul_2(1, 1)
+    mul_3(0, 1)
+    rs_second(0)
+    ag_fourth(1, 1)
+    mul_3(1, 1)
+    row_sums(1)
+    rs_third(0)
+    rs_first(1)
+    spread_sums(1)
     rs_second(1)
-    move_second(0)
-    grad_up(1)
+    finish(0, totals_of(0))
+
     rs_third(1)
-    routed[...] = place_rows(0)
-    grad_up(2)
-    grad_up(3)
-    finish(1)
-    move_second(1)
-    routed[...] += place_rows(1)
-    columns = pl.ds(pl.multiple_of(q_me * CHIP, CHIP), CHIP)
-    for i in range(7):
-        stage[i] = routed[i * SLOT : (i + 1) * SLOT].astype(BF16)
-        send(stage.at[i], landed.at[:, columns], put_send.at[i], put_recv.at[i], mate(i))
-    landed[:, columns] = routed[7 * SLOT :].astype(BF16)
-    for i in range(7):
-        there = landed.at[:, pl.ds(pl.multiple_of(mate_from(i) * CHIP, CHIP), CHIP)]
-        recv(there, put_send.at[i], put_recv.at[i])
+    for j in range(3):
+        move_second(0, j)
+    totals = totals_of(1)
+    for j in range(3):
+        routed[:, starts[j] : starts[j] + 2 * WIDTHS[j]] = place_rows(0, j)
+    finish(1, totals, 0)
+    move_second(1, 0)
+    move_second(1, 1)
+    put_part(0)
+    move_second(1, 2)
+    put_part(1)
+    put_part(2)
+    for k in range(4):
+        grad_up(k)
+    for j in range(3):
+        wait_part(j)
     returned_ref[...] = landed[...]
 
     for h in range(2):
@@ -551,7 +631,8 @@
 
         @pl.when(s > 0)
         def _():
-            move_copy(h).wait_send()
+            for j in range(3):
+                move_copy(h, j).wait_send()
 
     for copy in sends:
         copy.wait_send()
@@ -585,10 +666,10 @@
             both(lambda t: pltpu.VMEM((CHIPS, LOCAL, t), BF16)),
             both(lambda t: pltpu.VMEM((LOCAL, t), BF16)),
             both(lambda t: pltpu.VMEM((2, LOCAL, t), BF16)),
-            both(lambda t: pltpu.VMEM((2, PART, t), BF16)),
+            both(lambda t: pltpu.VMEM((2, LOCAL, t), BF16)),
             both(lambda t: pltpu.VMEM((2, LOCAL, t), BF16)),
             both(lambda t: pltpu.VMEM((LOCAL, t), BF16)),
-            both(lambda t: pltpu.VMEM((2, PIECE, t), BF16)),
+            both(lambda t: pltpu.VMEM((2, LOCAL, t), BF16)),
             pltpu.VMEM((LOCAL, ROWS), BF16),
             pltpu.VMEM((LOCAL, ROWS), BF16),
             pltpu.VMEM((LOCAL, ROWS), F32),
@@ -599,11 +680,12 @@
             both(lambda t: pltpu.VMEM((8, t), F32)),
             both(lambda t: pltpu.VMEM((CHIPS, 8, t), F32)),
             pltpu.VMEM((16, CHIP), BF16),
+            pltpu.VMEM((LOCAL, 128), F32),
             both(lambda t: pltpu.VMEM((LOCAL, t), BF16)),
             both(lambda t: pltpu.VMEM((CHIP, t), BF16)),
             pltpu.VMEM((CHIPS * SLOT, ROWS), BF16),
             pltpu.VMEM((CHIPS * SLOT, CHIP), F32),
-            pltpu.VMEM((7, SLOT, CHIP), BF16),
+            tuple(pltpu.VMEM((CHIPS * SLOT, 2 * w), BF16) for w in WIDTHS),
             pltpu.VMEM((SLOT, D), BF16),
             dma((4, N_AG)),
             dma((4, N_AG)),
@@ -613,16 +695,16 @@
             dma((2, 8)),
             dma((2, CHIPS)),
             dma((2, CHIPS)),
-            dma((2, N_RS)),
-            dma((2, N_RS)),
-            dma((2, 2)),
-            dma((2, 2)),
-            dma((7,)),
-            dma((7,)),
+            dma((4 * N_RS,)),
+            dma((4 * N_RS,)),
+            dma((2, 6)),
+            dma((2, 6)),
+            dma((7, 6)),
+            dma((7, 6)),
             dma((4,)),
         ],
         compiler_params=pltpu.CompilerParams(
-            collective_id=0, has_side_effects=True, vmem_limit_bytes=48 * MIB
+            collective_id=0, has_side_effects=True, vmem_limit_bytes=50 * MIB
         ),
         cost_estimate=pl.CostEstimate(
             flops=8 * ROWS * D * CHIP, bytes_accessed=20 * MIB, transcendentals=2 * ROWS * CHIP

time: 103 us -> 96 us (0.932)
  Pallas kernels: 97 us -> 90.9 us
    pallas_call x1, Pallas kernels: 97 us -> 90.9 us  [layer(): pl.pallas_call(layer_kernel, out_shape=[pltpu.VMEM((D, CHIP), BF16), pltp...]
where the time goes in v3:
time: 96 us; the launch traced here: 95.9 us
  Pallas kernels  90.9 us (95%)
  local copies, waits for them, and re-layouts  3.63 us (4%)
  between operations  1.29 us (1%)
    pallas_call x1, Pallas kernels, layer(): pl.pallas_call(layer_kernel, out_shape=[pltpu.VMEM((D, CHIP), BF16), pltp...  90.9 us
    unnamed x2, local copies, waits for them, and re-layouts  3.63 us

profile of v3, /device:TPU:7, one launch (start us, length us, event | category | flops | bytes accessed | tf_op | source)
XLA Modules:
  0.0 95.9 jit_solution(5419072306162880445)
XLA Ops:
  1.3 90.9 %shard_map.86 = (bf16[5120,640]{1,0:T(8,128)(2,1)S(1)}, bf16[64,5120]{1,0:T(8,128)(2,1)S(1)}) custom-call(bf16[320,512]{1,0:T(8,128)(2,1)} %bitcast.5, bf16[320,512]{1,0:T(8,128)(2,1)} %bitcast.6, bf16[1,320]{1,0:T(2,128)(2,1)} %gain_ref.1, s32[1]{0:T(128)S(6)} %copy.13.live_ref, s32[128]{0:T(128)} %bitcast.7, bf16[1,5120,640]{2,1,0:T(8,128)(2,1)} %wu_hbm.1, ...), custom_call_target="tpu_custom_call" | custom-call | flops 13421772800 | bytes 20971520 | tf_op jit(solution)/shard_map/pallas_call | solution.py:649
  92.2 2.8 %copy.11 = bf16[1,5120,640]{2,1,0:T(8,128)(2,1)} copy(bf16[1,5120,640]{2,1,0:T(8,128)(2,1)S(1)} %bitcast.4) | data formatting | bytes 13107200
  95.0 0.8 copy.12

commit v4 on v3

--- a/solution.py
+++ b/solution.py
@@ -23,7 +23,7 @@
 HEAD, TAIL = (0, PART), (PART, PART)
 FIRST, BUT_FIRST = (0, PIECE), (PIECE, LOCAL - PIECE)
 LAST, BUT_LAST = (LOCAL - PIECE, PIECE), (0, LOCAL - PIECE)
-PARTS = (((LOCAL, PIECE),), ((LOCAL, PIECE),))
+PARTS = (((LOCAL, 16),), ((LOCAL, 16),))
 WIDTHS = (128, 128, 64)
 GU = 1280
 MIB = 2**20
@@ -575,10 +575,10 @@
     ag_across(0, 1)
     ag_across(1, 1)
     mul_1(1, 0)
+    ag_third(0, 0)
     mul_1(0, 1)
-    ag_third(0, 0)
+    ag_third(1, 0)
     mul_1(1, 1)
-    ag_third(1, 0)
     mul_2(0, 0)
     mul_2(1, 0)
     ag_fourth(0, 0)

time: 96 us -> 94.9 us (0.989)
  Pallas kernels: 90.9 us -> 89.7 us
    pallas_call x1, Pallas kernels: 90.9 us -> 89.7 us  [layer(): pl.pallas_call(layer_kernel, out_shape=[pltpu.VMEM((D, CHIP), BF16), pltp...]
where the time goes in v4:
time: 94.9 us; the launch traced here: 94.6 us
  Pallas kernels  89.7 us (95%)
  local copies, waits for them, and re-layouts  3.63 us (4%)
  between operations  1.29 us (1%)
    pallas_call x1, Pallas kernels, layer(): pl.pallas_call(layer_kernel, out_shape=[pltpu.VMEM((D, CHIP), BF16), pltp...  89.7 us
    unnamed x2, local copies, waits for them, and re-layouts  3.63 us

profile of v4, /device:TPU:7, one launch (start us, length us, event | category | flops | bytes accessed | tf_op | source)
XLA Modules:
  0.0 94.6 jit_solution(11917864161840240839)
XLA Ops:
  1.3 89.7 %shard_map.86 = (bf16[5120,640]{1,0:T(8,128)(2,1)S(1)}, bf16[64,5120]{1,0:T(8,128)(2,1)S(1)}) custom-call(bf16[320,512]{1,0:T(8,128)(2,1)} %bitcast.5, bf16[320,512]{1,0:T(8,128)(2,1)} %bitcast.6, bf16[1,320]{1,0:T(2,128)(2,1)} %gain_ref.1, s32[1]{0:T(128)S(6)} %copy.13.live_ref, s32[128]{0:T(128)} %bitcast.7, bf16[1,5120,640]{2,1,0:T(8,128)(2,1)} %wu_hbm.1, ...), custom_call_target="tpu_custom_call" | custom-call | flops 13421772800 | bytes 20971520 | tf_op jit(solution)/shard_map/pallas_call | solution.py:649
  90.9 2.8 %copy.11 = bf16[1,5120,640]{2,1,0:T(8,128)(2,1)} copy(bf16[1,5120,640]{2,1,0:T(8,128)(2,1)S(1)} %bitcast.4) | data formatting | bytes 13107200
  93.7 0.8 copy.12
